TPU v7x, 256 devices: a whole 4x4x8 slice. The times are simulated.
256 devices in a mesh: seq: 32 (over z_hi, x, core), fsdp: 8 (over z_lo, y).
Axes of the slice: x: 4, y: 4, z: 8 (z_hi: 4, z_lo: 2; z = z_hi * 2 + z_lo), core: 2. Of those that a mesh axis runs over, the one named last changes fastest.
Arguments:
- activations: bfloat16 [65536, 2048], P('seq', 'fsdp'), may hold values from -3 to 3
- mix_first: bfloat16 [256, 256], replicated, may hold values from -0.375 to 0.375
- twiddle: float32 [256, 256], P('seq'), may hold values from 0.4 to 2
- mix_second: bfloat16 [256, 256], replicated, may hold values from -0.375 to 0.375
- up_first: bfloat16 [8, 256, 256], P('fsdp'), may hold values from -0.375 to 0.375
- up_second: bfloat16 [8, 256, 1024], P('fsdp'), may hold values from -0.375 to 0.375
- down_first: bfloat16 [8, 1024, 256], P('fsdp'), may hold values from -0.1875 to 0.1875
- down_second: bfloat16 [8, 256, 256], P('fsdp'), may hold values from -0.375 to 0.375
- grad_out: bfloat16 [65536, 2048], P('seq', 'fsdp'), may hold values from -3 to 3
Outputs:
- output: bfloat16 [65536, 2048], P('seq', 'fsdp')
- grad_inputs: bfloat16 [65536, 2048], P('seq', 'fsdp')
- grad_up_first: float32 [8, 256, 256], P('fsdp')
- grad_up_second: float32 [8, 256, 1024], P('fsdp')
- grad_down_first: float32 [8, 1024, 256], P('fsdp')
- grad_down_second: float32 [8, 256, 256], P('fsdp')
All inputs are finite; a program needn't handle non-finite values.
Results may differ from a plain program's by a relative error of at most 0.01.
Values may be sent and summed in bfloat16 or wider, within the bound.
A program may use at most 128 MiB of HBM per device.

v0:
```python
import jax
import jax.numpy as jnp
from jax import lax
from jax.sharding import PartitionSpec as P

root_two_pi = 0.7978845608028654
cubic_term = 0.044715


def gelu_value(values):
    inner = root_two_pi * (values + cubic_term * values * values * values)
    return 0.5 * values * (1.0 + jnp.tanh(inner))


def gelu_slope(values):
    inner = root_two_pi * (values + cubic_term * values * values * values)
    hyper = jnp.tanh(inner)
    return 0.5 * (1.0 + hyper) + 0.5 * values * (1.0 - hyper * hyper) * root_two_pi * (
        1.0 + 3.0 * cubic_term * values * values
    )


def product(form, left, right):
    return jnp.einsum(form, left, right, preferred_element_type=jnp.float32)


def column_pass(field, factor):
    result = product(
        "ajc,ai->ijc", lax.all_to_all(field, "seq", split_axis=1, concat_axis=0, tiled=True), factor
    ).astype(jnp.bfloat16)
    return lax.all_to_all(result, "seq", split_axis=0, concat_axis=1, tiled=True)


def permute_blocks(values):
    count, blocks, width = values.shape
    stride = width // blocks
    return jnp.transpose(values.reshape(count, blocks, blocks, stride), (0, 2, 3, 1)).reshape(
        count, blocks, width
    )


def unpermute_blocks(values):
    count, blocks, width = values.shape
    stride = width // blocks
    return jnp.transpose(values.reshape(count, blocks, stride, blocks), (0, 3, 1, 2)).reshape(
        count, blocks, width
    )


def whole_layer(hidden_rows, grad_rows, up_first, up_second, down_first, down_second):
    count = hidden_rows.shape[0]
    blocks, width = (up_first.shape[0], up_first.shape[1])
    hidden_three = hidden_rows.reshape(count, blocks, width)
    up_mid = product("tkp,kpq->tkq", hidden_three, up_first).astype(jnp.bfloat16)
    up_perm = permute_blocks(up_mid)
    pre_act = product("tge,geo->tgo", up_perm, up_second)
    activated = gelu_value(pre_act).astype(jnp.bfloat16)
    down_mid = product("tgo,goq->tgq", activated, down_first).astype(jnp.bfloat16)
    down_perm = permute_blocks(down_mid)
    down_out = product("tge,geq->tgq", down_perm, down_second).reshape(count, blocks * width)
    output_rows = (hidden_rows.astype(jnp.float32) + down_out).astype(jnp.bfloat16)
    grad_three = grad_rows.reshape(count, blocks, width)
    sum_down_second = product("tge,tgq->geq", down_perm, grad_three)
    back_perm = product("tgq,geq->tge", grad_three, down_second).astype(jnp.bfloat16)
    back_mid = unpermute_blocks(back_perm)
    sum_down_first = product("tgo,tgq->goq", activated, back_mid)
    grad_act = product("tgq,goq->tgo", back_mid, down_first)
    grad_pre = (grad_act * gelu_slope(pre_act)).astype(jnp.bfloat16)
    sum_up_second = product("tge,tgo->geo", up_perm, grad_pre)
    grad_perm = product("tgo,geo->tge", grad_pre, up_second).astype(jnp.bfloat16)
    grad_mid = unpermute_blocks(grad_perm)
    sum_up_first = product("tkp,tkq->kpq", hidden_three, grad_mid)
    grad_inner = product("tkq,kpq->tkp", grad_mid, up_first).reshape(count, blocks * width)
    grad_hidden = (grad_rows.astype(jnp.float32) + grad_inner).astype(jnp.bfloat16)
    return (
        output_rows,
        grad_hidden,
        (sum_up_first, sum_up_second, sum_down_first, sum_down_second),
    )


def shards(
    activations,
    mix_first,
    twiddle,
    mix_second,
    up_first,
    up_second,
    down_first,
    down_second,
    grad_out,
):
    local_rows, local_channels = activations.shape
    block_rows = twiddle.shape[0]
    length = mix_first.shape[0]
    inputs_three = activations.reshape(block_rows, length, local_channels)
    first_pass = (product("abc,bj->ajc", inputs_three, mix_first) * twiddle[:, :, None]).astype(
        jnp.bfloat16
    )
    mixed = column_pass(first_pass, mix_second).reshape(local_rows, local_channels)
    inputs_float = activations.astype(jnp.float32)
    gating = jax.nn.sigmoid(inputs_float)
    mixed_float = mixed.astype(jnp.float32)
    hidden = (inputs_float + gating * mixed_float).astype(jnp.bfloat16)
    token_hidden, token_grad = (
        lax.all_to_all(hidden, "fsdp", split_axis=0, concat_axis=1, tiled=True),
        lax.all_to_all(grad_out, "fsdp", split_axis=0, concat_axis=1, tiled=True),
    )
    weights = (
        lax.all_gather(up_first, "fsdp", axis=0, tiled=True),
        lax.all_gather(up_second, "fsdp", axis=0, tiled=True),
        lax.all_gather(down_first, "fsdp", axis=0, tiled=True),
        lax.all_gather(down_second, "fsdp", axis=0, tiled=True),
    )
    token_output, token_back, full_grads = whole_layer(
        token_hidden, token_grad, weights[0], weights[1], weights[2], weights[3]
    )
    output, grad_hidden = (
        lax.all_to_all(token_output, "fsdp", split_axis=1, concat_axis=0, tiled=True),
        lax.all_to_all(token_back, "fsdp", split_axis=1, concat_axis=0, tiled=True),
    )
    grads = (
        lax.psum_scatter(full_grads[0], "fsdp", scatter_dimension=0, tiled=True),
        lax.psum_scatter(full_grads[1], "fsdp", scatter_dimension=0, tiled=True),
        lax.psum_scatter(full_grads[2], "fsdp", scatter_dimension=0, tiled=True),
        lax.psum_scatter(full_grads[3], "fsdp", scatter_dimension=0, tiled=True),
    )
    totals = lax.psum((grads[0], grads[1], grads[2], grads[3]), "seq")
    grad_float = grad_hidden.astype(jnp.float32)
    grad_mixed = (grad_float * gating).astype(jnp.bfloat16)
    back_rows = column_pass(grad_mixed.reshape(block_rows, length, local_channels), mix_second.T)
    twisted = (back_rows.astype(jnp.float32) * twiddle[:, :, None]).astype(jnp.bfloat16)
    mix_grad = product("ajc,bj->abc", twisted, mix_first).reshape(local_rows, local_channels)
    grad_inputs = (grad_float * (1.0 + gating * (1.0 - gating) * mixed_float) + mix_grad).astype(
        jnp.bfloat16
    )
    scale = 1.0 / length
    return (
        output,
        grad_inputs,
        totals[0] * scale,
        totals[1] * scale,
        totals[2] * scale,
        totals[3] * scale,
    )


def solution(mesh):
    in_specs = (
        P("seq", "fsdp"),
        P(),
        P("seq", None),
        P(),
        P("fsdp", None, None),
        P("fsdp", None, None),
        P("fsdp", None, None),
        P("fsdp", None, None),
        P("seq", "fsdp"),
    )
    out_specs = (
        P("seq", "fsdp"),
        P("seq", "fsdp"),
        P("fsdp", None, None),
        P("fsdp", None, None),
        P("fsdp", None, None),
        P("fsdp", None, None),
    )
    return jax.shard_map(shards, mesh=mesh, in_specs=in_specs, out_specs=out_specs, check_vma=False)
```

profile of v0, /device:TPU:1, one launch (start us, length us, event | category | flops | bytes accessed | tf_op | source)
XLA Modules:
  0.0 896.8 jit_solution(5252346037619965176)
XLA Ops:
  12.7 12.6 %all-to-all-start = ((bf16[8,256,256]{2,0,1:T(8,128)(2,1)}), bf16[8,256,256]{2,0,1:T(8,128)(2,1)S(1)}, u32[]{:S(2)}, u32[]{:S(2)}) async-start(bf16[8,256,256]{2,0,1:T(8,128)(2,1)} %copy.106), calls=%async_computation | async-start | bytes 2097152 | tf_op jit(solution)/shard_map/all_to_all | solution.py:29
  25.8 36.8 %all-to-all-done = bf16[8,256,256]{2,0,1:T(8,128)(2,1)S(1)} async-done(((bf16[8,256,256]{2,0,1:T(8,128)(2,1)}), bf16[8,256,256]{2,0,1:T(8,128)(2,1)S(1)}, u32[]{:S(2)}, u32[]{:S(2)}) %all-to-all-start) | async-done | bytes 1048608 | tf_op jit(solution)/shard_map/all_to_all | solution.py:29
  64.5 37.9 %all_to_all.112 = bf16[256,8,256]{2,1,0:T(8,128)(2,1)S(1)} all-to-all(bf16[256,8,256]{2,1,0:T(8,128)(2,1)S(1)} %copy.110), channel_id=1, replica_groups=mesh['seq'=32,'fsdp'=8] {'seq'}, dimensions={0} | all-to-all | bytes 2097152 | tf_op jit(solution)/shard_map/all_to_all | solution.py:31
  102.4 5.7 all-to-all-start.4
  111.1 12.0 %all-to-all-done.4 = bf16[8,256,256]{2,1,0:T(8,128)(2,1)S(1)} async-done(((bf16[8,256,256]{2,1,0:T(8,128)(2,1)}), bf16[8,256,256]{2,1,0:T(8,128)(2,1)S(1)}, u32[]{:S(2)}, u32[]{:S(2)}) %all-to-all-start.4) | async-done | bytes 1048608 | tf_op jit(solution)/shard_map/all_to_all | solution.py:107
  123.1 4.2 all-to-all-start.2
  130.2 17.1 %all-to-all-done.2 = bf16[8,256,256]{2,1,0:T(8,128)(2,1)} async-done(((bf16[8,256,256]{2,1,0:T(8,128)(2,1)}), bf16[8,256,256]{2,1,0:T(8,128)(2,1)}, u32[]{:S(2)}, u32[]{:S(2)}) %all-to-all-start.2) | async-done | bytes 1048608 | tf_op jit(solution)/shard_map/all_to_all | solution.py:106
  149.3 34.5 %all-gather.7.cloned.1.call-done = bf16[8,256,1024]{2,1,0:T(8,128)(2,1)} async-done(((bf16[1,256,1024]{2,1,0:T(8,128)(2,1)}), bf16[8,256,1024]{2,1,0:T(8,128)(2,1)}) %all-gather.7.cloned.1.call-update) | async-done | bytes 4194320 | tf_op jit(solution)/shard_map/all_gather | solution.py:111
  183.9 7.0 fusion.32
  190.9 44.8 %all-gather.9.cloned.1.call-done = bf16[8,1024,256]{2,1,0:T(8,128)(2,1)} async-done(((bf16[1,1024,256]{2,1,0:T(8,128)(2,1)}), bf16[8,1024,256]{2,1,0:T(8,128)(2,1)}) %all-gather.9.cloned.1.call-update) | async-done | bytes 4194320 | tf_op jit(solution)/shard_map/all_gather | solution.py:112
  235.7 9.6 %fusion.6 = bf16[256,8,1024]{2,0,1:T(8,128)(2,1)S(1)} fusion(f32[8,256,1024]{2,1,0:T(8,128)} %fusion.32, bf16[8,1024,256]{2,1,0:T(8,128)(2,1)} %all-gather.9.cloned.1.call-done, bf16[256,8,256]{0,1,2:T(8,128)(2,1)} %bitcast.162), kind=kOutput, calls=%fused_computation.8 | convolution fusion | flops 1113587712 | bytes 17825792 | tf_op jit(solution)/shard_map/tgq,goq->tgo/dot_general | solution.py:24
  251.7 8.2 convolution_convert_fusion.3
  263.1 6.9 fusion.30
  271.3 10.0 %fusion.42 = f32[8,1024,256]{2,1,0:T(8,128)} fusion(bf16[256,8,256]{0,1,2:T(8,128)(2,1)S(1)} %bitcast.163, f32[8,256,1024]{2,1,0:T(8,128)} %fusion.32), kind=kOutput, calls=%fused_computation.62 | convolution fusion | flops 1092616192 | bytes 17825792 | tf_op jit(solution)/shard_map/tgo,tgq->goq/dot_general | solution.py:24
  283.9 18.3 %all_to_all.113 = bf16[256,8,256]{2,0,1:T(8,128)(2,1)S(1)} all-to-all(bf16[256,8,256]{2,0,1:T(8,128)(2,1)S(1)} %fusion.18), channel_id=1, replica_groups=mesh['seq'=32,'fsdp'=8] {'fsdp'}, dimensions={1} | all-to-all | bytes 2097152 | tf_op jit(solution)/shard_map/all_to_all | solution.py:120
  305.3 10.6 %all-to-all-start.6 = ((bf16[8,256,256]{2,0,1:T(8,128)(2,1)}), bf16[8,256,256]{2,0,1:T(8,128)(2,1)}, u32[]{:S(2)}, u32[]{:S(2)}) async-start(bf16[8,256,256]{2,0,1:T(8,128)(2,1)} %copy.122), calls=%async_computation.6 | async-start | bytes 2097152 | tf_op jit(solution)/shard_map/all_to_all | solution.py:29
  315.9 3.7 fusion.19
  319.6 35.6 %all-to-all-done.6 = bf16[8,256,256]{2,0,1:T(8,128)(2,1)} async-done(((bf16[8,256,256]{2,0,1:T(8,128)(2,1)}), bf16[8,256,256]{2,0,1:T(8,128)(2,1)}, u32[]{:S(2)}, u32[]{:S(2)}) %all-to-all-start.6) | async-done | bytes 1048608 | tf_op jit(solution)/shard_map/all_to_all | solution.py:29
  355.2 4.2 all-to-all-start.3
  365.2 9.9 %all-to-all-done.3 = bf16[256,8,256]{2,0,1:T(8,128)(2,1)} async-done(((bf16[256,8,256]{2,0,1:T(8,128)(2,1)}), bf16[256,8,256]{2,0,1:T(8,128)(2,1)}, u32[]{:S(2)}, u32[]{:S(2)}) %all-to-all-start.3) | async-done | bytes 1048608 | tf_op jit(solution)/shard_map/all_to_all | solution.py:119
  375.1 8.5 all-to-all-start.7
  383.7 104.5 %reduce-scatter.7.cloned.1.call-done = f32[1,256,1024]{2,1,0:T(8,128)} async-done(((f32[8,256,1024]{2,1,0:T(8,128)}), f32[1,256,1024]{2,1,0:T(8,128)}) %reduce-scatter.7.cloned.1.call-update) | async-done | bytes 1048592 | tf_op jit(solution)/shard_map/reduce_scatter | solution.py:124
  488.3 97.7 %reduce-scatter.9.cloned.1.call-done = f32[1,1024,256]{2,1,0:T(8,128)} async-done(((f32[8,1024,256]{2,1,0:T(8,128)}), f32[1,1024,256]{2,1,0:T(8,128)}) %reduce-scatter.9.cloned.1.call-update) | async-done | bytes 1048592 | tf_op jit(solution)/shard_map/reduce_scatter | solution.py:125
  591.1 291.4 %all-reduce.3.cloned.1.call-done = (f32[1,256,256]{2,1,0:T(8,128)}, f32[1,256,1024]{2,1,0:T(8,128)}, f32[1,1024,256]{2,1,0:T(8,128)}, f32[1,256,256]{2,1,0:T(8,128)}) async-done(((f32[1,256,256]{2,1,0:T(8,128)}, f32[1,256,1024]{2,1,0:T(8,128)}, f32[1,1024,256]{2,1,0:T(8,128)}, f32[1,256,256]{2,1,0:T(8,128)}), (f32[1,256,256]{2,1,0:T(8,128)}, f32[1,256,1024]{2,1,0:T(8,128)}, f32[1,1024,256]{2,1,0:T(8,128)}, ...) | async-done | bytes 2621456 | tf_op jit(solution)/shard_map/psum | solution.py:128
  (78 shorter events, 50.7 us)
Async XLA Ops:
  7.2 55.8 %copy-start = (bf16[256,256]{1,0:T(8,128)(2,1)S(1)}, bf16[256,256]{1,0:T(8,128)(2,1)}, u32[]{:S(2)}) copy-start(bf16[256,256]{1,0:T(8,128)(2,1)} %param.12) | copy-start | bytes 393220
  7.2 120.4 %all-gather.11.cloned.1.call-start = ((), (), s32[]{:S(2)}) async-start(), calls=%async_computation.15 | async-start | bytes 1179648 | tf_op jit(solution)/shard_map/all_gather | solution.py:113
  7.9 122.3 %all-gather.5.cloned.1.call-start = ((), (), s32[]{:S(2)}) async-start(), calls=%async_computation.12 | async-start | bytes 1179648 | tf_op jit(solution)/shard_map/all_gather | solution.py:110
  8.7 175.2 %all-gather.7.cloned.1.call-start = ((), (), s32[]{:S(2)}) async-start(), calls=%async_computation.13 | async-start | bytes 4718592 | tf_op jit(solution)/shard_map/all_gather | solution.py:111
  12.7 50.0 %all-to-all-start = ((bf16[8,256,256]{2,0,1:T(8,128)(2,1)}), bf16[8,256,256]{2,0,1:T(8,128)(2,1)S(1)}, u32[]{:S(2)}, u32[]{:S(2)}) async-start(bf16[8,256,256]{2,0,1:T(8,128)(2,1)} %copy.106), calls=%async_computation | async-start | bytes 2097152 | tf_op jit(solution)/shard_map/all_to_all | solution.py:29
  25.2 210.4 %all-gather.9.cloned.1.call-start = ((), (), s32[]{:S(2)}) async-start(), calls=%async_computation.14 | async-start | bytes 4718592 | tf_op jit(solution)/shard_map/all_gather | solution.py:112
  102.4 20.6 %all-to-all-start.4 = ((bf16[8,256,256]{2,1,0:T(8,128)(2,1)}), bf16[8,256,256]{2,1,0:T(8,128)(2,1)S(1)}, u32[]{:S(2)}, u32[]{:S(2)}) async-start(bf16[8,256,256]{2,1,0:T(8,128)(2,1)} %bitcast.164), calls=%async_computation.4 | async-start | bytes 2097152 | tf_op jit(solution)/shard_map/all_to_all | solution.py:107
  123.1 7.2 copy-start.3
  123.1 24.2 %all-to-all-start.2 = ((bf16[8,256,256]{2,1,0:T(8,128)(2,1)}), bf16[8,256,256]{2,1,0:T(8,128)(2,1)}, u32[]{:S(2)}, u32[]{:S(2)}) async-start(bf16[8,256,256]{2,1,0:T(8,128)(2,1)} %bitcast.157), calls=%async_computation.2 | async-start | bytes 2097152 | tf_op jit(solution)/shard_map/all_to_all | solution.py:106
  127.3 256.4 %reduce-scatter.5.cloned.1.call-start = ((), (), s32[]{:S(2)}) async-start(), calls=%async_computation.16 | async-start | bytes 2359296 | tf_op jit(solution)/shard_map/reduce_scatter | solution.py:123
  235.7 9.6 %copy-start.5 = (bf16[8,256,1024]{2,1,0:T(8,128)(2,1)S(1)}, bf16[8,256,1024]{2,1,0:T(8,128)(2,1)}, u32[]{:S(2)}) copy-start(bf16[8,256,1024]{2,1,0:T(8,128)(2,1)} %all-gather.7.cloned.1.call-done) | copy-start | bytes 12582916
  251.4 132.3 %reduce-scatter.11.cloned.1.call-start = ((), (), s32[]{:S(2)}) async-start(), calls=%async_computation.19 | async-start | bytes 2359296 | tf_op jit(solution)/shard_map/reduce_scatter | solution.py:126
  251.7 9.2 %copy-start.4 = (bf16[8,256,256]{2,1,0:T(8,128)(2,1)S(1)}, bf16[8,256,256]{2,1,0:T(8,128)(2,1)}, u32[]{:S(2)}) copy-start(bf16[8,256,256]{2,1,0:T(8,128)(2,1)} %copy-done.3) | copy-start | bytes 3145732
  263.1 225.2 %reduce-scatter.7.cloned.1.call-start = ((), (), s32[]{:S(2)}) async-start(), calls=%async_computation.17 | async-start | bytes 9437184 | tf_op jit(solution)/shard_map/reduce_scatter | solution.py:124
  270.1 315.9 %reduce-scatter.9.cloned.1.call-start = ((), (), s32[]{:S(2)}) async-start(), calls=%async_computation.18 | async-start | bytes 9437184 | tf_op jit(solution)/shard_map/reduce_scatter | solution.py:125
  281.3 21.8 %copy-start.2 = (bf16[2048,256]{1,0:T(8,128)(2,1)S(1)}, bf16[2048,256]{1,0:T(8,128)(2,1)}, u32[]{:S(2)}) copy-start(bf16[2048,256]{1,0:T(8,128)(2,1)} %param.9) | copy-start | bytes 3145732
  305.3 49.9 %all-to-all-start.6 = ((bf16[8,256,256]{2,0,1:T(8,128)(2,1)}), bf16[8,256,256]{2,0,1:T(8,128)(2,1)}, u32[]{:S(2)}, u32[]{:S(2)}) async-start(bf16[8,256,256]{2,0,1:T(8,128)(2,1)} %copy.122), calls=%async_computation.6 | async-start | bytes 2097152 | tf_op jit(solution)/shard_map/all_to_all | solution.py:29
  355.2 19.8 %all-to-all-start.3 = ((bf16[256,8,256]{2,0,1:T(8,128)(2,1)}), bf16[256,8,256]{2,0,1:T(8,128)(2,1)}, u32[]{:S(2)}, u32[]{:S(2)}) async-start(bf16[256,8,256]{2,0,1:T(8,128)(2,1)} %fusion.19), calls=%async_computation.3 | async-start | bytes 2097152 | tf_op jit(solution)/shard_map/all_to_all | solution.py:119
  361.0 225.0 %copy-start.11 = (bf16[256,256]{1,0:T(8,128)(2,1)S(1)}, bf16[256,256]{1,0:T(8,128)(2,1)}, u32[]{:S(2)}) copy-start(bf16[256,256]{1,0:T(8,128)(2,1)} %param.10) | copy-start | bytes 393220
  361.0 225.0 %copy-start.14 = (f32[8,256]{1,0:T(8,128)S(1)}, f32[8,256]{1,0:T(8,128)}, u32[]{:S(2)}) copy-start(f32[8,256]{1,0:T(8,128)} %param.11) | copy-start | bytes 24580
  375.1 210.9 %all-to-all-start.7 = ((bf16[256,8,256]{2,1,0:T(8,128)(2,1)}), bf16[256,8,256]{2,1,0:T(8,128)(2,1)}, u32[]{:S(2)}, u32[]{:S(2)}) async-start(bf16[256,8,256]{2,1,0:T(8,128)(2,1)} %copy.126), calls=%async_computation.7 | async-start | bytes 2097152 | tf_op jit(solution)/shard_map/all_to_all | solution.py:31
  383.6 498.9 %all-reduce.3.cloned.1.call-start = ((), (), s32[]{:S(2)}) async-start(), calls=%async_computation.20 | async-start | bytes 5242880 | tf_op jit(solution)/shard_map/psum | solution.py:128
  882.5 4.6 copy-start.12
  882.5 4.6 copy-start.13
  (6 other events, 7.4 us)
Sparse Core Ops, SparseCore 0:
  9.8 50.6 all-gather.10
  62.3 48.5 all-gather.4
  112.6 71.1 all-gather.6
  185.5 50.1 all-gather.8
  251.6 38.5 reduce-scatter.4
  292.6 71.0 reduce-scatter.10
  366.3 121.9 reduce-scatter.6
  490.8 95.1 reduce-scatter.8
  588.9 293.6 all-reduce.2
where the time goes:
time: 898 us; the launch traced here: 897 us
  waiting for transfers between devices  687 us (77%)
  matrix products  64.8 us (7%)
  blocking collectives  56.2 us (6%)
  starting transfers between devices  46.7 us (5%)
  local copies, waits for them, and re-layouts  16.7 us (2%)
  between operations  14.1 us (2%)
  other arithmetic  11.3 us (1%)
    psum x1, waiting for transfers between devices, shards(): totals = lax.psum((grads[0], grads[1], grads[2], grads[3]), 'seq')  291 us
    reduce_scatter x1, waiting for transfers between devices, shards(): lax.psum_scatter(full_grads[1], 'fsdp', scatter_dimension=0, tiled=True)  105 us
    reduce_scatter x1, waiting for transfers between devices, shards(): lax.psum_scatter(full_grads[2], 'fsdp', scatter_dimension=0, tiled=True)  97.7 us
    all_to_all x2, waiting for transfers between devices, column_pass(): lax.all_to_all(field, 'seq', split_axis=1, concat_axis=0, tiled=True)  72.4 us
    dot_general x16, matrix products, product(): return jnp.einsum(form, left, right, preferred_element_type=jnp.float32)  64.8 us
    all_gather x1, waiting for transfers between devices, shards(): lax.all_gather(down_first, 'fsdp', axis=0, tiled=True)  44.8 us
    all_to_all x1, blocking collectives, column_pass(): lax.all_to_all(result, 'seq', split_axis=0, concat_axis=1, tiled=True)  37.9 us
    all_gather x1, waiting for transfers between devices, shards(): lax.all_gather(up_second, 'fsdp', axis=0, tiled=True)  34.5 us
  transfers between devices with their start and end apart: 15, of which 10 were waited for; matrix products, arithmetic and copies ran while one was open for 7% of the time, Pallas kernels for 0%

commit v1 on v0

v1 whole, which is shorter than its diff:
```python
import jax
import jax.numpy as jnp
from jax import lax
from jax.sharding import PartitionSpec as P

root_two_pi = 0.7978845608028654
cubic_term = 0.044715


def gelu_both(values):
    square = values * values
    hyper = jnp.tanh(root_two_pi * values * (1.0 + cubic_term * square))
    half = 0.5 * (1.0 + hyper)
    slope = half + 0.5 * values * (1.0 - hyper * hyper) * root_two_pi * (1.0 + 3.0 * cubic_term * square)
    return values * half, slope


def product(form, left, right):
    return jnp.einsum(form, left, right, preferred_element_type=jnp.float32)


def column_pass(field, factor):
    result = product(
        "ajc,ai->ijc", lax.all_to_all(field, "seq", split_axis=1, concat_axis=0, tiled=True), factor
    ).astype(jnp.bfloat16)
    return lax.all_to_all(result, "seq", split_axis=0, concat_axis=1, tiled=True)


def swap_blocks(rows):
    return lax.all_to_all(rows, "fsdp", split_axis=0, concat_axis=0, tiled=True)


def shards(activations, mix_first, twiddle, mix_second, up_first, up_second, down_first, down_second, grad_out):
    bf16 = jnp.bfloat16
    local_rows, local_channels = activations.shape
    block_rows = twiddle.shape[0]
    length = mix_first.shape[0]
    width = up_first.shape[1]
    units = up_second.shape[2]
    blocks = lax.axis_size("fsdp")
    members = lax.axis_size("seq")
    stride = width // blocks
    first, second, third, fourth = up_first[0], up_second[0], down_first[0], down_second[0]
    second = second.reshape(stride, blocks, units).transpose(1, 0, 2).reshape(width, units)
    fourth = fourth.reshape(stride, blocks, width).transpose(1, 0, 2).reshape(width, width)
    back_mid = swap_blocks(product("tq,eq->et", grad_out, fourth).astype(bf16))

    inputs_three = activations.reshape(block_rows, length, local_channels)
    first_pass = (product("abc,bj->ajc", inputs_three, mix_first) * twiddle[:, :, None]).astype(bf16)
    mixed = column_pass(first_pass, mix_second).reshape(local_rows, local_channels)
    inputs_float = activations.astype(jnp.float32)
    gating = jax.nn.sigmoid(inputs_float)
    mixed_float = mixed.astype(jnp.float32)
    hidden = (inputs_float + gating * mixed_float).astype(bf16)

    up_perm = swap_blocks(product("tp,pq->qt", hidden, first).astype(bf16))
    pre_act = product("eo,et->ot", second, up_perm)
    value, slope = gelu_both(pre_act)
    activated = value.astype(bf16)
    down_perm = swap_blocks(product("oq,ot->qt", third, activated).astype(bf16))
    output = (hidden.astype(jnp.float32) + product("et,eq->tq", down_perm, fourth)).astype(bf16)
    grad_pre = (product("oq,qt->ot", third, back_mid) * slope).astype(bf16)
    grad_mid = swap_blocks(product("eo,ot->et", second, grad_pre).astype(bf16))
    grad_inner = product("qt,pq->tp", grad_mid, first)
    grad_hidden = (grad_out.astype(jnp.float32) + grad_inner).astype(bf16)

    terms = jnp.concatenate(
        (
            product("qt,tp->qp", grad_mid, hidden).astype(bf16),
            product("ot,et->oe", grad_pre, up_perm).astype(bf16),
            product("ot,qt->oq", activated, back_mid).astype(bf16),
            product("et,tq->eq", down_perm, grad_out).astype(bf16),
        )
    )
    terms = lax.all_to_all(terms, "seq", split_axis=0, concat_axis=0, tiled=True)
    owned = jnp.sum(terms.reshape(members, -1, width).astype(jnp.float32), axis=0).astype(bf16)
    totals = lax.all_gather(owned, "seq", axis=0, tiled=True).astype(jnp.float32) * (1.0 / length)

    grad_float = grad_hidden.astype(jnp.float32)
    grad_mixed = (grad_float * gating).astype(bf16)
    back_rows = column_pass(grad_mixed.reshape(block_rows, length, local_channels), mix_second.T)
    twisted = (back_rows.astype(jnp.float32) * twiddle[:, :, None]).astype(bf16)
    mix_grad = product("ajc,bj->abc", twisted, mix_first).reshape(local_rows, local_channels)
    grad_inputs = (grad_float * (1.0 + gating * (1.0 - gating) * mixed_float) + mix_grad).astype(bf16)

    sum_first = totals[:width].T
    sum_second = totals[width : width + units].T.reshape(blocks, stride, units).transpose(1, 0, 2).reshape(width, units)
    sum_third = totals[width + units : width + 2 * units]
    sum_fourth = totals[width + 2 * units :].reshape(blocks, stride, width).transpose(1, 0, 2).reshape(width, width)
    return (output, grad_inputs, sum_first[None], sum_second[None], sum_third[None], sum_fourth[None])


def solution(mesh):
    block = P("fsdp", None, None)
    in_specs = (P("seq", "fsdp"), P(), P("seq", None), P(), block, block, block, block, P("seq", "fsdp"))
    out_specs = (P("seq", "fsdp"), P("seq", "fsdp"), block, block, block, block)
    return jax.shard_map(shards, mesh=mesh, in_specs=in_specs, out_specs=out_specs, check_vma=False)
```

time: 898 us -> 333 us (0.37)
  waiting for transfers between devices: 687 us -> 126 us
  blocking collectives: 56.2 us -> 75.1 us
  matrix products: 64.8 us -> 48.7 us
    psum x1 -> x0, waiting for transfers between devices: 291 us -> none  [shards(): totals = lax.psum((grads[0], grads[1], grads[2], grads[3]), 'seq')]
    reduce_scatter x4 -> x0, waiting for transfers between devices: 202 us -> none  [the longest x1 105 us: shards(): lax.psum_scatter(full_grads[1], 'fsdp', scatter_dimension=0, tiled=True)]
    all_to_all x2 -> x1, waiting for transfers between devices: 72.4 us -> 12.9 us  [column_pass(): lax.all_to_all(field, 'seq', split_axis=1, concat_axis=0, tiled=True)]
    all_gather x4 -> x1, waiting for transfers between devices: 79.3 us -> 32.8 us  [shards(): lax.all_gather(owned, 'seq', axis=0, tiled=True).astype(jnp.float32)]
    all_to_all x3 -> x5, waiting for transfers between devices: 38.9 us -> 61.5 us  [the longest x4 39.2 us: swap_blocks(): return lax.all_to_all(rows, 'fsdp', split_axis=0, concat_axis=0, tiled=True)]
    all_to_all x1, blocking collectives: 18.3 us -> 40.1 us  [column_pass(): lax.all_to_all(field, 'seq', split_axis=1, concat_axis=0, tiled=True)]
    all_to_all x1, waiting for transfers between devices: 0.01 us -> 18.6 us  [column_pass(): lax.all_to_all(result, 'seq', split_axis=0, concat_axis=1, tiled=True)]
    all_to_all x2 -> x1, starting transfers between devices: 23.2 us -> 5.08 us  [column_pass(): lax.all_to_all(field, 'seq', split_axis=1, concat_axis=0, tiled=True)]
  transfers between devices with their start and end apart: 15 -> 8, of which waited for: 10 -> 8; matrix products, arithmetic and copies ran while one was open for 7% -> 14% of each run, Pallas kernels for 0% -> 0%
where the time goes in v1:
time: 333 us; the launch traced here: 332 us
  waiting for transfers between devices  126 us (38%)
  blocking collectives  75.1 us (23%)
  matrix products  48.7 us (15%)
  starting transfers between devices  44.2 us (13%)
  local copies, waits for them, and re-layouts  17.3 us (5%)
  between operations  14.4 us (4%)
  other arithmetic  6.4 us (2%)
    dot_general x16, matrix products, product(): return jnp.einsum(form, left, right, preferred_element_type=jnp.float32)  48.7 us
    all_to_all x1, blocking collectives, column_pass(): lax.all_to_all(field, 'seq', split_axis=1, concat_axis=0, tiled=True)  40.1 us
    all_to_all x4, waiting for transfers between devices, swap_blocks(): return lax.all_to_all(rows, 'fsdp', split_axis=0, concat_axis=0, tiled=True)  39.2 us
    all_to_all x1, blocking collectives, column_pass(): lax.all_to_all(result, 'seq', split_axis=0, concat_axis=1, tiled=True)  35 us
    all_gather x1, waiting for transfers between devices, shards(): lax.all_gather(owned, 'seq', axis=0, tiled=True).astype(jnp.float32)  32.8 us
    all_to_all x1, waiting for transfers between devices, shards(): lax.all_to_all(terms, 'seq', split_axis=0, concat_axis=0, tiled=True)  22.3 us
    all_to_all x1, waiting for transfers between devices, column_pass(): lax.all_to_all(result, 'seq', split_axis=0, concat_axis=1, tiled=True)  18.6 us
    all_to_all x4, starting transfers between devices, swap_blocks(): return lax.all_to_all(rows, 'fsdp', split_axis=0, concat_axis=0, tiled=True)  17.2 us
  transfers between devices with their start and end apart: 8, of which 8 were waited for; matrix products, arithmetic and copies ran while one was open for 14% of the time, Pallas kernels for 0%

profile of v1, /device:TPU:1, one launch (start us, length us, event | category | flops | bytes accessed | tf_op | source)
XLA Modules:
  0.0 332.0 jit_solution(12740618201727484713)
XLA Ops:
  9.5 40.1 %all_to_all.111 = bf16[8,256,256]{2,0,1:T(8,128)(2,1)S(1)} all-to-all(bf16[8,256,256]{2,0,1:T(8,128)(2,1)S(1)} %copy.84), channel_id=1, replica_groups=mesh['seq'=32,'fsdp'=8] {'seq'}, dimensions={1} | all-to-all | bytes 2097152 | tf_op jit(solution)/shard_map/all_to_all | solution.py:24
  51.5 35.0 %all_to_all.112 = bf16[256,8,256]{2,1,0:T(8,128)(2,1)S(1)} all-to-all(bf16[256,8,256]{2,1,0:T(8,128)(2,1)S(1)} %copy.88), channel_id=1, replica_groups=mesh['seq'=32,'fsdp'=8] {'seq'}, dimensions={0} | all-to-all | bytes 2097152 | tf_op jit(solution)/shard_map/all_to_all | solution.py:26
  91.1 4.3 %all-to-all-start.2 = ((bf16[8,32,2048]{2,1,0:T(8,128)(2,1)}), bf16[8,32,2048]{2,1,0:T(8,128)(2,1)}, u32[]{:S(2)}, u32[]{:S(2)}) async-start(bf16[8,32,2048]{2,1,0:T(8,128)(2,1)} %bitcast.178), calls=%async_computation.2 | async-start | bytes 2097152 | tf_op jit(solution)/shard_map/all_to_all | solution.py:30
  95.5 2.7 convolution_convert_fusion.1
  98.2 12.7 %all-to-all-done.2 = bf16[8,32,2048]{2,1,0:T(8,128)(2,1)} async-done(((bf16[8,32,2048]{2,1,0:T(8,128)(2,1)}), bf16[8,32,2048]{2,1,0:T(8,128)(2,1)}, u32[]{:S(2)}, u32[]{:S(2)}) %all-to-all-start.2) | async-done | bytes 1048608 | tf_op jit(solution)/shard_map/all_to_all | solution.py:30
  110.9 4.3 %all-to-all-start.4 = ((bf16[8,32,2048]{2,1,0:T(8,128)(2,1)}), bf16[8,32,2048]{2,1,0:T(8,128)(2,1)}, u32[]{:S(2)}, u32[]{:S(2)}) async-start(bf16[8,32,2048]{2,1,0:T(8,128)(2,1)} %bitcast.177), calls=%async_computation.4 | async-start | bytes 2097152 | tf_op jit(solution)/shard_map/all_to_all | solution.py:30
  116.3 7.4 %fusion.3 = (bf16[1024,2048]{0,1:T(8,128)(2,1)}, f32[2048,1024,1]{1,0,2:T(8,128)}) fusion(bf16[8,32,2048]{2,1,0:T(8,128)(2,1)} %all-to-all-done.2, bf16[32,8,1024]{2,1,0:T(8,128)(2,1)S(1)} %bitcast.190), kind=kOutput, calls=%fused_computation.8 | convolution fusion | flops 1092616192 | bytes 14155776 | tf_op jit(solution)/shard_map/eo,et->ot/dot_general | solution.py:19
  123.7 6.5 %all-to-all-done.4 = bf16[8,32,2048]{2,1,0:T(8,128)(2,1)} async-done(((bf16[8,32,2048]{2,1,0:T(8,128)(2,1)}), bf16[8,32,2048]{2,1,0:T(8,128)(2,1)}, u32[]{:S(2)}, u32[]{:S(2)}) %all-to-all-start.4) | async-done | bytes 1048608 | tf_op jit(solution)/shard_map/all_to_all | solution.py:30
  130.2 7.9 %fusion = bf16[1024,2048]{0,1:T(8,128)(2,1)S(1)} fusion(f32[2048,1024,1]{1,0,2:T(8,128)} %get-tuple-element.41, bf16[256,2048]{1,0:T(8,128)(2,1)} %bitcast.28, bf16[1,1024,256]{2,1,0:T(8,128)(2,1)S(1)} %copy-done), kind=kOutput, calls=%fused_computation.1 | convolution fusion | flops 1111490560 | bytes 14155776 | tf_op jit(solution)/shard_map/oq,qt->ot/dot_general | solution.py:19
  140.5 4.4 %all-to-all-start.5 = ((bf16[8,32,2048]{2,1,0:T(8,128)(2,1)}), bf16[8,32,2048]{2,1,0:T(8,128)(2,1)}, u32[]{:S(2)}, u32[]{:S(2)}) async-start(bf16[8,32,2048]{2,1,0:T(8,128)(2,1)} %bitcast.184), calls=%async_computation.5 | async-start | bytes 2097152 | tf_op jit(solution)/shard_map/all_to_all | solution.py:30
  144.9 4.5 %convolution_convert_fusion.2 = bf16[2048,256]{0,1:T(8,128)(2,1)} fusion(bf16[1024,2048]{0,1:T(8,128)(2,1)} %get-tuple-element.40, bf16[1,1024,256]{2,1,0:T(8,128)(2,1)S(1)} %copy-done), kind=kOutput, calls=%fused_computation.27 | convolution fusion | flops 1074266112 | bytes 5767168 | tf_op jit(solution)/shard_map/oq,ot->qt/dot_general | solution.py:19
  149.4 10.3 %all-to-all-done.5 = bf16[8,32,2048]{2,1,0:T(8,128)(2,1)} async-done(((bf16[8,32,2048]{2,1,0:T(8,128)(2,1)}), bf16[8,32,2048]{2,1,0:T(8,128)(2,1)}, u32[]{:S(2)}, u32[]{:S(2)}) %all-to-all-start.5) | async-done | bytes 1048608 | tf_op jit(solution)/shard_map/all_to_all | solution.py:30
  159.7 4.3 %all-to-all-start.3 = ((bf16[8,32,2048]{2,1,0:T(8,128)(2,1)}), bf16[8,32,2048]{2,1,0:T(8,128)(2,1)}, u32[]{:S(2)}, u32[]{:S(2)}) async-start(bf16[8,32,2048]{2,1,0:T(8,128)(2,1)} %bitcast.183), calls=%async_computation.3 | async-start | bytes 2097152 | tf_op jit(solution)/shard_map/all_to_all | solution.py:30
  163.9 3.7 %fusion.17 = (bf16[2048,256]{1,0:T(8,128)(2,1)S(1)}, bf16[2048,256]{1,0:T(8,128)(2,1)}) fusion(bf16[2048,256]{1,0:T(8,128)(2,1)} %param.9, bf16[256,2048]{1,0:T(8,128)(2,1)} %bitcast.33, bf16[1,256,256]{2,1,0:T(8,128)(2,1)S(1)} %copy-done.10, bf16[2048,256]{1,0:T(8,128)(2,1)} %param.17), kind=kOutput, calls=%fused_computation.35 | convolution fusion | flops 273678336 | bytes 5373952 | tf_op jit(solution)/shard_map/qt,pq->tp/dot_general | solution.py:19
  169.2 9.7 %all-to-all-done.3 = bf16[8,32,2048]{2,1,0:T(8,128)(2,1)} async-done(((bf16[8,32,2048]{2,1,0:T(8,128)(2,1)}), bf16[8,32,2048]{2,1,0:T(8,128)(2,1)}, u32[]{:S(2)}, u32[]{:S(2)}) %all-to-all-start.3) | async-done | bytes 1048608 | tf_op jit(solution)/shard_map/all_to_all | solution.py:30
  178.8 5.1 %all-to-all-start.6 = ((bf16[8,256,256]{2,0,1:T(8,128)(2,1)}), bf16[8,256,256]{2,0,1:T(8,128)(2,1)}, u32[]{:S(2)}, u32[]{:S(2)}) async-start(bf16[8,256,256]{2,0,1:T(8,128)(2,1)} %copy.92), calls=%async_computation.6 | async-start | bytes 2097152 | tf_op jit(solution)/shard_map/all_to_all | solution.py:24
  183.9 4.0 %convolution_convert_fusion.6 = bf16[1024,256]{1,0:T(8,128)(2,1)S(1)} fusion(bf16[1024,2048]{0,1:T(8,128)(2,1)} %get-tuple-element.40, bf16[256,2048]{1,0:T(8,128)(2,1)} %bitcast.28), kind=kOutput, calls=%fused_computation.50 | convolution fusion | flops 1074003968 | bytes 5767168 | tf_op jit(solution)/shard_map/ot,qt->oq/dot_general | solution.py:19
  195.2 12.9 %all-to-all-done.6 = bf16[8,256,256]{2,0,1:T(8,128)(2,1)} async-done(((bf16[8,256,256]{2,0,1:T(8,128)(2,1)}), bf16[8,256,256]{2,0,1:T(8,128)(2,1)}, u32[]{:S(2)}, u32[]{:S(2)}) %all-to-all-start.6) | async-done | bytes 1048608 | tf_op jit(solution)/shard_map/all_to_all | solution.py:24
  208.1 10.0 %all-to-all-start.8 = ((bf16[32,80,256]{2,1,0:T(8,128)(2,1)}), bf16[32,80,256]{2,1,0:T(8,128)(2,1)}, u32[]{:S(2)}, u32[]{:S(2)}) async-start(bf16[32,80,256]{2,1,0:T(8,128)(2,1)} %bitcast.175), calls=%async_computation.8 | async-start | bytes 2621440 | tf_op jit(solution)/shard_map/all_to_all | solution.py:75
  223.8 22.3 %all-to-all-done.8 = bf16[32,80,256]{2,1,0:T(8,128)(2,1)} async-done(((bf16[32,80,256]{2,1,0:T(8,128)(2,1)}), bf16[32,80,256]{2,1,0:T(8,128)(2,1)}, u32[]{:S(2)}, u32[]{:S(2)}) %all-to-all-start.8) | async-done | bytes 1310752 | tf_op jit(solution)/shard_map/all_to_all | solution.py:75
  246.1 11.7 %all-to-all-start.7 = ((bf16[256,8,256]{2,1,0:T(8,128)(2,1)}), bf16[256,8,256]{2,1,0:T(8,128)(2,1)}, u32[]{:S(2)}, u32[]{:S(2)}) async-start(bf16[256,8,256]{2,1,0:T(8,128)(2,1)} %copy.96), calls=%async_computation.7 | async-start | bytes 2097152 | tf_op jit(solution)/shard_map/all_to_all | solution.py:26
  260.2 3.0 fusion.9
  263.2 18.6 %all-to-all-done.7 = bf16[256,8,256]{2,1,0:T(8,128)(2,1)} async-done(((bf16[256,8,256]{2,1,0:T(8,128)(2,1)}), bf16[256,8,256]{2,1,0:T(8,128)(2,1)}, u32[]{:S(2)}, u32[]{:S(2)}) %all-to-all-start.7) | async-done | bytes 1048608 | tf_op jit(solution)/shard_map/all_to_all | solution.py:26
  285.6 32.8 %all-gather.2.cloned.1.call-done = bf16[2560,256]{1,0:T(8,128)(2,1)} async-done(((bf16[80,256]{1,0:T(8,128)(2,1)}), bf16[2560,256]{1,0:T(8,128)(2,1)}) %all-gather.2.cloned.1.call-update) | async-done | bytes 1310736 | tf_op jit(solution)/shard_map/all_gather | solution.py:77
  (65 shorter events, 39.6 us)
Async XLA Ops:
  7.2 123.0 %copy-start = (bf16[1,1024,256]{2,1,0:T(8,128)(2,1)S(1)}, bf16[1,1024,256]{2,1,0:T(8,128)(2,1)}, u32[]{:S(2)}) copy-start(bf16[1,1024,256]{2,1,0:T(8,128)(2,1)} %param.15) | copy-start | bytes 1572868
  9.5 40.4 %copy-start.11 = (bf16[256,256]{1,0:T(8,128)(2,1)S(1)}, bf16[256,256]{1,0:T(8,128)(2,1)}, u32[]{:S(2)}) copy-start(bf16[256,256]{1,0:T(8,128)(2,1)} %param.12) | copy-start | bytes 393220
  86.7 1.2 copy-start.1
  88.0 1.7 copy-start.10
  88.7 1.0 copy-start.3
  89.7 5.7 %copy-start.12 = (bf16[1,256,256]{2,1,0:T(8,128)(2,1)S(1)}, bf16[1,256,256]{2,1,0:T(8,128)(2,1)}, u32[]{:S(2)}) copy-start(bf16[1,256,256]{2,1,0:T(8,128)(2,1)} %param.16) | copy-start | bytes 393220
  91.1 19.8 %all-to-all-start.2 = ((bf16[8,32,2048]{2,1,0:T(8,128)(2,1)}), bf16[8,32,2048]{2,1,0:T(8,128)(2,1)}, u32[]{:S(2)}, u32[]{:S(2)}) async-start(bf16[8,32,2048]{2,1,0:T(8,128)(2,1)} %bitcast.178), calls=%async_computation.2 | async-start | bytes 2097152 | tf_op jit(solution)/shard_map/all_to_all | solution.py:30
  95.4 19.8 %copy-start.8 = (bf16[1,256,1024]{2,1,0:T(8,128)(2,1)S(1)}, bf16[1,256,1024]{2,1,0:T(8,128)(2,1)}, u32[]{:S(2)}) copy-start(bf16[1,256,1024]{2,1,0:T(8,128)(2,1)} %param.14) | copy-start | bytes 1572868
  110.9 19.3 %all-to-all-start.4 = ((bf16[8,32,2048]{2,1,0:T(8,128)(2,1)}), bf16[8,32,2048]{2,1,0:T(8,128)(2,1)}, u32[]{:S(2)}, u32[]{:S(2)}) async-start(bf16[8,32,2048]{2,1,0:T(8,128)(2,1)} %bitcast.177), calls=%async_computation.4 | async-start | bytes 2097152 | tf_op jit(solution)/shard_map/all_to_all | solution.py:30
  130.2 8.0 %copy-start.9 = (bf16[32,8,1024]{2,0,1:T(8,128)(2,1)S(1)}, bf16[32,8,1024]{2,0,1:T(8,128)(2,1)}, u32[]{:S(2)}) copy-start(bf16[32,8,1024]{2,0,1:T(8,128)(2,1)} %copy.90) | copy-start | bytes 1572868
  138.1 2.4 copy-start.14
  140.5 19.2 %all-to-all-start.5 = ((bf16[8,32,2048]{2,1,0:T(8,128)(2,1)}), bf16[8,32,2048]{2,1,0:T(8,128)(2,1)}, u32[]{:S(2)}, u32[]{:S(2)}) async-start(bf16[8,32,2048]{2,1,0:T(8,128)(2,1)} %bitcast.184), calls=%async_computation.5 | async-start | bytes 2097152 | tf_op jit(solution)/shard_map/all_to_all | solution.py:30
  159.7 19.2 %all-to-all-start.3 = ((bf16[8,32,2048]{2,1,0:T(8,128)(2,1)}), bf16[8,32,2048]{2,1,0:T(8,128)(2,1)}, u32[]{:S(2)}, u32[]{:S(2)}) async-start(bf16[8,32,2048]{2,1,0:T(8,128)(2,1)} %bitcast.183), calls=%async_computation.3 | async-start | bytes 2097152 | tf_op jit(solution)/shard_map/all_to_all | solution.py:30
  178.8 29.3 %all-to-all-start.6 = ((bf16[8,256,256]{2,0,1:T(8,128)(2,1)}), bf16[8,256,256]{2,0,1:T(8,128)(2,1)}, u32[]{:S(2)}, u32[]{:S(2)}) async-start(bf16[8,256,256]{2,0,1:T(8,128)(2,1)} %copy.92), calls=%async_computation.6 | async-start | bytes 2097152 | tf_op jit(solution)/shard_map/all_to_all | solution.py:24
  183.9 4.0 %copy-start.15 = (bf16[1024,2048]{0,1:T(8,128)(2,1)S(1)}, bf16[1024,2048]{0,1:T(8,128)(2,1)}, u32[]{:S(2)}) copy-start(bf16[1024,2048]{0,1:T(8,128)(2,1)} %copy-done.14) | copy-start | bytes 12582916
  187.9 2.7 copy-start.4
  187.9 4.4 %copy-start.5 = (bf16[2048,256]{1,0:T(8,128)(2,1)S(1)}, bf16[2048,256]{1,0:T(8,128)(2,1)}, u32[]{:S(2)}) copy-start(bf16[2048,256]{1,0:T(8,128)(2,1)} %param.17) | copy-start | bytes 3145732
  208.1 37.9 %all-to-all-start.8 = ((bf16[32,80,256]{2,1,0:T(8,128)(2,1)}), bf16[32,80,256]{2,1,0:T(8,128)(2,1)}, u32[]{:S(2)}, u32[]{:S(2)}) async-start(bf16[32,80,256]{2,1,0:T(8,128)(2,1)} %bitcast.175), calls=%async_computation.8 | async-start | bytes 2621440 | tf_op jit(solution)/shard_map/all_to_all | solution.py:75
  246.1 35.8 %all-to-all-start.7 = ((bf16[256,8,256]{2,1,0:T(8,128)(2,1)}), bf16[256,8,256]{2,1,0:T(8,128)(2,1)}, u32[]{:S(2)}, u32[]{:S(2)}) async-start(bf16[256,8,256]{2,1,0:T(8,128)(2,1)} %copy.96), calls=%async_computation.7 | async-start | bytes 2097152 | tf_op jit(solution)/shard_map/all_to_all | solution.py:26
  257.7 60.7 %all-gather.2.cloned.1.call-start = ((), (), s32[]{:S(2)}) async-start(), calls=%async_computation.9 | async-start | bytes 1351680 | tf_op jit(solution)/shard_map/all_gather | solution.py:77
  260.2 21.6 %copy-start.7 = (bf16[256,256]{1,0:T(8,128)(2,1)S(1)}, bf16[256,256]{1,0:T(8,128)(2,1)}, u32[]{:S(2)}) copy-start(bf16[256,256]{1,0:T(8,128)(2,1)} %param.10) | copy-start | bytes 393220
  260.2 21.6 %copy-start.13 = (f32[8,256]{1,0:T(8,128)S(1)}, f32[8,256]{1,0:T(8,128)}, u32[]{:S(2)}) copy-start(f32[8,256]{1,0:T(8,128)} %param.11) | copy-start | bytes 24580
  281.8 1.9 copy-start.2
  281.8 2.0 copy-start.6
Sparse Core Ops, SparseCore 0:
  261.7 56.6 all-gather.1

commit v2 on v1

v2 whole, which is shorter than its diff:
```python
import functools

import jax
import jax.numpy as jnp
from jax import lax
from jax.experimental import pallas as pl
from jax.experimental.pallas import tpu as pltpu
from jax.sharding import PartitionSpec as P

MESH = pl.DeviceIdType.MESH
bf16, f32 = jnp.bfloat16, jnp.float32
root_two_pi = 0.7978845608028654
cubic_term = 0.044715
CHUNKS = 2
A1, A2, A3, A4 = range(4)
BACK, UP, GRAD, DOWN = range(4)


def gelu_both(values):
    square = values * values
    hyper = jnp.tanh(root_two_pi * values * (1.0 + cubic_term * square))
    half = 0.5 * (1.0 + hyper)
    slope = half + 0.5 * values * (1.0 - hyper * hyper) * root_two_pi * (1.0 + 3.0 * cubic_term * square)
    return values * half, slope


def nn(left, right):
    return lax.dot_general(left, right, (((1,), (0,)), ((), ())), preferred_element_type=f32)


def nt(left, right):
    return lax.dot_general(left, right, (((1,), (1,)), ((), ())), preferred_element_type=f32)


def tn(left, right):
    return lax.dot_general(left, right, (((0,), (0,)), ((), ())), preferred_element_type=f32)


def layer(
    act_rows, act, gout, mix_in, mix_out, mix_fwd, mix_bwd, tw,
    first_t, second, second_t, third, third_t, fourth,
    out, grad_in, total,
    wide, extra, field_s, field_r, swap_s, swap_r, hidden, active, gpre, acc, send_terms, half_in, half_sum,
    quarter_in, quarter_sum, last_in,
    seq_send, seq_recv, swap_send, swap_recv, red_send, red_recv,
):
    s = lax.axis_index("seq")
    f = lax.axis_index("fsdp")
    zh, xx, core = s // 8, (s // 2) % 4, s % 2
    zl, yy = f // 4, f % 4
    rows = field_s.shape[3]
    span = swap_s.shape[3]

    def seq_peer(dz, n):
        return ((zh + dz) % 4 * 4 + (xx + n // 2) % 4) * 2 + (core + n) % 2

    def swap_peer(n):
        return (zl + n // 4) % 2 * 4 + (yy + n) % 4

    barrier = pltpu.get_barrier_semaphore()

    def greet(peer_seq, peer_fsdp):
        pl.semaphore_signal(barrier, inc=1, device_id={"seq": peer_seq, "fsdp": peer_fsdp}, device_id_type=MESH)

    @pl.loop(1, 32)
    def _(n):
        greet((s + n) % 32, f)

    @pl.loop(1, 8)
    def _(n):
        greet(s, (f + n) % 8)

    def seq_start(phase, q):
        pltpu.make_async_copy(field_s.at[phase, q, s], field_r.at[phase, q, s], seq_recv.at[phase, q]).start()
        for dz in (2, 1, 3, 0):
            @pl.loop(1 if dz == 0 else 0, 8)
            def _(n):
                peer = seq_peer(dz, n)
                pltpu.make_async_remote_copy(
                    src_ref=field_s.at[phase, q, peer], dst_ref=field_r.at[phase, q, s],
                    send_sem=seq_send.at[phase, q], recv_sem=seq_recv.at[phase, q],
                    device_id={"seq": peer, "fsdp": f}, device_id_type=MESH,
                ).start()

    def seq_wait(phase, q):
        whole = field_r.at[phase, q]
        pltpu.make_async_copy(whole, whole, seq_recv.at[phase, q]).wait()

    def swap_start(phase, q):
        own = pl.ds(pl.multiple_of(f * 32, 32), 32)
        pltpu.make_async_copy(swap_s.at[phase, q, own], swap_r.at[phase, q, own], swap_recv.at[phase, q]).start()

        @pl.loop(1, 8)
        def _(n):
            peer = swap_peer(8 - n)
            pltpu.make_async_remote_copy(
                src_ref=swap_s.at[phase, q, pl.ds(pl.multiple_of(peer * 32, 32), 32)], dst_ref=swap_r.at[phase, q, own],
                send_sem=swap_send.at[phase, q], recv_sem=swap_recv.at[phase, q],
                device_id={"seq": s, "fsdp": peer}, device_id_type=MESH,
            ).start()

    def swap_wait(phase, q):
        whole = swap_r.at[phase, q]
        pltpu.make_async_copy(whole, whole, swap_recv.at[phase, q]).wait()

    for a in range(8):
        lines = nn(mix_in[...], act_rows[a]) * tw[:, a : a + 1]
        for half in range(2):
            wide[half, pl.ds(a, 256, stride=8), :] = lines[:, half * 128 : half * 128 + 128]
    for q in range(CHUNKS):
        @pl.loop(0, 32)
        def _(d):
            for half in range(2):
                place = pl.ds(pl.multiple_of(q * 32 * rows + d * rows, 8), rows)
                field_s[A1, q, d, :, half * 128 : half * 128 + 128] = wide[half, place, :].astype(bf16)

    pl.semaphore_wait(barrier, 38)
    for q in range(CHUNKS):
        seq_start(A1, q)

    tile = 256
    tiles = span // tile

    def token_tile(t):
        return pl.ds(pl.multiple_of(t * tile, tile), tile)

    def field_tile(ref, phase, q, t):
        per = tile // rows
        return ref.at[phase, q, pl.ds(t * per, per)]

    for q in range(CHUNKS):
        @pl.loop(0, tiles)
        def _(t):
            swap_s[BACK, q, :, token_tile(t)] = nt(fourth[...], gout[q, token_tile(t), :]).astype(bf16)
        swap_start(BACK, q)

    def mix_columns(source, target, factor, q):
        for pair in range(rows // 16):
            part = pl.ds(pair * 16, 16)
            block = field_r[source, q, :, part, :].astype(f32).reshape(32, 2, 8, 256)
            mixed = [nn(factor[...], block[:, k].reshape(256, 256).astype(bf16)).reshape(32, 8, 256) for k in range(2)]
            field_s[target, q, :, part, :] = jnp.stack(mixed, axis=1).reshape(32, 16, 256).astype(bf16)

    def gate(q, t):
        return act[q, token_tile(t), :].astype(f32)

    for q in range(CHUNKS):
        seq_wait(A1, q)
        mix_columns(A1, A2, mix_fwd, q)
        seq_start(A2, q)

    for q in range(CHUNKS):
        seq_wait(A2, q)

        @pl.loop(0, tiles)
        def _(t):
            inputs = gate(q, t)
            mixed = field_tile(field_r, A2, q, t)[...].reshape(tile, 256).astype(f32)
            rows_hidden = (inputs + jax.nn.sigmoid(inputs) * mixed).astype(bf16)
            hidden[q, token_tile(t), :] = rows_hidden
            swap_s[UP, q, :, token_tile(t)] = nt(first_t[...], rows_hidden).astype(bf16)
        swap_start(UP, q)

    for q in range(CHUNKS):
        if q == 0:
            for other in range(CHUNKS):
                swap_wait(BACK, other)
        swap_wait(UP, q)

        @pl.loop(0, tiles)
        def _(t):
            columns = token_tile(t)
            up = swap_r[UP, q, :, columns]
            back = swap_r[BACK, q, :, columns]

            @pl.loop(0, 4)
            def _(o):
                units = pl.ds(pl.multiple_of(o * 256, 256), 256)
                value, slope = gelu_both(nn(second_t[units, :], up))
                active[q, units, columns] = value.astype(bf16)
                gpre[q, units, columns] = (nn(third[units, :], back) * slope).astype(bf16)
            swap_s[GRAD, q, :, columns] = nn(second[...], gpre[q, :, columns]).astype(bf16)
            swap_s[DOWN, q, :, columns] = nn(third_t[...], active[q, :, columns]).astype(bf16)
        swap_start(GRAD, q)
        swap_start(DOWN, q)

    for q in range(CHUNKS):
        swap_wait(GRAD, q)

        @pl.loop(0, tiles)
        def _(t):
            columns = token_tile(t)
            inner = tn(swap_r[GRAD, q, :, columns], first_t[...])
            back = (gout[q, columns, :].astype(f32) + inner).astype(bf16).astype(f32)
            gating = jax.nn.sigmoid(gate(q, t))
            mixed = field_tile(field_r, A2, q, t)[...].reshape(tile, 256).astype(f32)
            field_tile(field_s, A3, q, t)[...] = (back * gating).astype(bf16).reshape(tile // rows, rows, 256)
            rest = back * (1.0 + gating * (1.0 - gating) * mixed)
            for half in range(2):
                place = pl.ds(pl.multiple_of(q * span + t * tile, tile), tile)
                extra[half, place, :] = rest[:, half * 128 : half * 128 + 128]
        seq_start(A3, q)

    def add(place, values, q):
        if q == 0:
            acc[place, :] = values
        else:
            acc[place, :] += values

    for q in range(CHUNKS):
        @pl.loop(0, 4)
        def _(o):
            units = pl.ds(pl.multiple_of(o * 256, 256), 256)
            add(pl.ds(pl.multiple_of(256 + o * 256, 256), 256), nt(gpre[q, units, :], swap_r[UP, q]), q)
            add(pl.ds(pl.multiple_of(1280 + o * 256, 256), 256), nt(active[q, units, :], swap_r[BACK, q]), q)
        add(pl.ds(0, 256), nn(swap_r[GRAD, q], hidden[q]), q)

    for q in range(CHUNKS):
        swap_wait(DOWN, q)

        @pl.loop(0, tiles)
        def _(t):
            columns = token_tile(t)
            out[q, columns, :] = (hidden[q, columns, :].astype(f32) + tn(swap_r[DOWN, q, :, columns], fourth[...])).astype(bf16)
        add(pl.ds(2304, 256), nn(swap_r[DOWN, q], gout[q]), q)

    def core_peer():
        return {"seq": zh * 8 + xx * 2 + 1 - core, "fsdp": f}

    def x_peer(n):
        return {"seq": zh * 8 + (xx + n) % 4 * 2 + core, "fsdp": f}

    def z_peer(n):
        return {"seq": (zh + n) % 4 * 8 + xx * 2 + core, "fsdp": f}

    def red(stage, n, source, target, peer):
        return pltpu.make_async_remote_copy(
            src_ref=source, dst_ref=target, send_sem=red_send.at[stage, n], recv_sem=red_recv.at[stage, n],
            device_id=peer, device_id_type=MESH,
        )

    def rows_at(ref, start, count):
        return ref.at[pl.ds(pl.multiple_of(start, 16), count)]

    def reduce_core():
        @pl.loop(0, 10)
        def _(t):
            place = pl.ds(pl.multiple_of((1 - core) * 1280 + t * 128, 128), 128)
            send_terms[pl.ds(pl.multiple_of(t * 128, 128), 128), :] = acc[place, :].astype(bf16)
        copy = red(0, 0, send_terms, half_in, core_peer())
        copy.start()
        return [copy]

    def reduce_x():
        @pl.loop(0, 10)
        def _(t):
            place = pl.ds(pl.multiple_of(t * 128, 128), 128)
            own = acc[pl.ds(pl.multiple_of(core * 1280 + t * 128, 128), 128), :]
            half_sum[place, :] = (own + half_in[place, :].astype(f32)).astype(bf16)
        copies = [red(1, n - 1, rows_at(half_sum, (xx + n) % 4 * 320, 320), quarter_in.at[n - 1], x_peer(n)) for n in (2, 1, 3)]
        for copy in copies:
            copy.start()
        return copies

    def reduce_z():
        own = rows_at(half_sum, xx * 320, 320)[...].astype(f32)
        for n in range(3):
            own += quarter_in[n].astype(f32)
        quarter_sum[...] = own.astype(bf16)
        copies = [red(2, n - 1, rows_at(quarter_sum, (zh + n) % 4 * 80, 80), last_in.at[n - 1], z_peer(n)) for n in (2, 1, 3)]
        for copy in copies:
            copy.start()
        return copies

    def gather_z():
        own = rows_at(quarter_sum, zh * 80, 80)[...].astype(f32)
        for n in range(3):
            own += last_in[n].astype(f32)
        place = rows_at(total, core * 1280 + xx * 320 + zh * 80, 80)
        place[...] = own.astype(bf16)
        copies = [red(3, n - 1, place, place, z_peer(n)) for n in (2, 1, 3)]
        for copy in copies:
            copy.start()
        return copies

    def gather_x():
        place = rows_at(total, core * 1280 + xx * 320, 320)
        copies = [red(4, n - 1, place, place, x_peer(n)) for n in (2, 1, 3)]
        for copy in copies:
            copy.start()
        return copies

    def gather_core():
        place = rows_at(total, core * 1280, 1280)
        copy = red(5, 0, place, place, core_peer())
        copy.start()
        return [copy]

    def finish(copies):
        for copy in copies:
            copy.wait()

    copies = reduce_core()
    for q in range(CHUNKS):
        seq_wait(A3, q)
        mix_columns(A3, A4, mix_bwd, q)
        seq_start(A4, q)
        if q == 0:
            finish(copies)
            copies = reduce_x()
    finish(copies)
    finish(reduce_z())
    finish(gather_z())
    finish(gather_x())
    copies = gather_core()

    for q in range(CHUNKS):
        seq_wait(A4, q)

        @pl.loop(0, 32)
        def _(d):
            for half in range(2):
                place = pl.ds(pl.multiple_of(q * 32 * rows + d * rows, 8), rows)
                wide[half, place, :] = field_r[A4, q, d, :, half * 128 : half * 128 + 128].astype(f32)
    for a in range(8):
        lines = pl.ds(a, 256, stride=8)
        for half in range(2):
            twisted = (wide[half, lines, :] * tw[:, a : a + 1]).astype(bf16)
            grad_in[a, :, half * 128 : half * 128 + 128] = (extra[half, lines, :] + nn(mix_out[...], twisted)).astype(bf16)
    finish(copies)

    for q in range(CHUNKS):
        for phase in range(4):
            sent = field_s.at[phase, q, pl.ds(0, 31)]
            pltpu.make_async_copy(sent, sent, seq_send.at[phase, q]).wait()
            sent = swap_s.at[phase, q, pl.ds(0, 224)]
            pltpu.make_async_copy(sent, sent, swap_send.at[phase, q]).wait()


def shards(activations, mix_first, twiddle, mix_second, up_first, up_second, down_first, down_second, grad_out):
    per = 8 // CHUNKS
    span = 2048 // CHUNKS
    first, second, third, fourth = up_first[0], up_second[0], down_first[0], down_second[0]
    second = second.reshape(32, 8, 1024).transpose(1, 0, 2).reshape(256, 1024)
    fourth = fourth.reshape(32, 8, 256).transpose(1, 0, 2).reshape(256, 256)

    def reorder(values):
        return values.reshape(32, CHUNKS, per, -1).transpose(1, 0, 2, 3).reshape(256, -1)

    def token_order(values):
        return values.reshape(8, 32, CHUNKS, per, 256).transpose(2, 1, 3, 0, 4).reshape(CHUNKS, span, 256)

    mix_in = reorder(mix_first.T)
    mix_out = reorder(reorder(mix_first).T).T
    tw = reorder(twiddle.T)
    act_rows = activations.reshape(8, 256, 256)
    args = (
        act_rows, token_order(activations), token_order(grad_out), mix_in, mix_out, mix_second.T, mix_second, tw,
        first.T, second, second.T, third, third.T, fourth,
    )
    vmem = pl.BlockSpec(memory_space=pltpu.VMEM)
    rows = 64 // CHUNKS
    output, grad_in, total = pl.pallas_call(
        layer,
        name="monarch_layer",
        out_shape=(
            jax.ShapeDtypeStruct((CHUNKS, span, 256), bf16),
            jax.ShapeDtypeStruct((8, 256, 256), bf16),
            jax.ShapeDtypeStruct((2560, 256), bf16),
        ),
        in_specs=[vmem] * len(args),
        out_specs=(vmem,) * 3,
        scratch_shapes=[
            pltpu.VMEM((2, 2048, 128), f32),
            pltpu.VMEM((2, 2048, 128), f32),
            pltpu.VMEM((4, CHUNKS, 32, rows, 256), bf16),
            pltpu.VMEM((4, CHUNKS, 32, rows, 256), bf16),
            pltpu.VMEM((4, CHUNKS, 256, span), bf16),
            pltpu.VMEM((4, CHUNKS, 256, span), bf16),
            pltpu.VMEM((CHUNKS, span, 256), bf16),
            pltpu.VMEM((CHUNKS, 1024, span), bf16),
            pltpu.VMEM((CHUNKS, 1024, span), bf16),
            pltpu.VMEM((2560, 256), f32),
            pltpu.VMEM((1280, 256), bf16),
            pltpu.VMEM((1280, 256), bf16),
            pltpu.VMEM((1280, 256), bf16),
            pltpu.VMEM((3, 320, 256), bf16),
            pltpu.VMEM((320, 256), bf16),
            pltpu.VMEM((3, 80, 256), bf16),
            pltpu.SemaphoreType.DMA((4, CHUNKS)),
            pltpu.SemaphoreType.DMA((4, CHUNKS)),
            pltpu.SemaphoreType.DMA((4, CHUNKS)),
            pltpu.SemaphoreType.DMA((4, CHUNKS)),
            pltpu.SemaphoreType.DMA((6, 3)),
            pltpu.SemaphoreType.DMA((6, 3)),
        ],
        compiler_params=pltpu.CompilerParams(collective_id=0, has_side_effects=True, vmem_limit_bytes=60 << 20),
    )(*args)

    output = output.reshape(CHUNKS, 32, per, 8, 256).transpose(3, 1, 0, 2, 4).reshape(2048, 256)
    grad_in = grad_in.reshape(8, CHUNKS, 32, per, 256).transpose(0, 2, 1, 3, 4).reshape(2048, 256)
    totals = total.astype(f32) * (1.0 / 256)
    sum_first = totals[:256].T
    sum_second = totals[256:1280].T.reshape(8, 32, 1024).transpose(1, 0, 2).reshape(256, 1024)
    sum_third = totals[1280:2304]
    sum_fourth = totals[2304:].reshape(8, 32, 256).transpose(1, 0, 2).reshape(256, 256)
    return (output, grad_in, sum_first[None], sum_second[None], sum_third[None], sum_fourth[None])


def solution(mesh):
    block = P("fsdp", None, None)
    in_specs = (P("seq", "fsdp"), P(), P("seq", None), P(), block, block, block, block, P("seq", "fsdp"))
    out_specs = (P("seq", "fsdp"), P("seq", "fsdp"), block, block, block, block)
    return jax.shard_map(shards, mesh=mesh, in_specs=in_specs, out_specs=out_specs, check_vma=False)
```

time: 333 us -> 206 us (0.62)
  Pallas kernels: 0 us -> 178 us
  waiting for transfers between devices: 126 us -> 0 us
  blocking collectives: 75.1 us -> 0 us
  matrix products: 48.7 us -> 0 us
  starting transfers between devices: 44.2 us -> 0 us
  between operations: 14.4 us -> 0.82 us
  local copies, waits for them, and re-layouts: 17.3 us -> 26.7 us
  other arithmetic: 6.4 us -> 0.17 us
    pallas_call x0 -> x1, Pallas kernels: none -> 178 us  [shards(): pl.pallas_call(layer, name='monarch_layer', out_shape=(jax.ShapeDtypeStru...]
    all_to_all x7 -> x0, waiting for transfers between devices: 93 us -> none  [the longest x4 39.2 us: swap_blocks(): return lax.all_to_all(rows, 'fsdp', split_axis=0, concat_axis=0, tiled=True)]
    all_to_all x2 -> x0, blocking collectives: 75.1 us -> none  [the longest x1 40.1 us: column_pass(): lax.all_to_all(field, 'seq', split_axis=1, concat_axis=0, tiled=True)]
    dot_general x16 -> x0, matrix products: 48.7 us -> none  [product(): return jnp.einsum(form, left, right, preferred_element_type=jnp.float32)]
    all_to_all x7 -> x0, starting transfers between devices: 43.9 us -> none  [the longest x4 17.2 us: swap_blocks(): return lax.all_to_all(rows, 'fsdp', split_axis=0, concat_axis=0, tiled=True)]
    all_gather x1 -> x0, waiting for transfers between devices: 32.8 us -> none  [shards(): lax.all_gather(owned, 'seq', axis=0, tiled=True).astype(jnp.float32)]
    reshape x1 -> x16, local copies, waits for them, and re-layouts: 1.56 us -> 11.9 us  [the longest x4 5.79 us: token_order(): values.reshape(8, 32, CHUNKS, per, 256).transpose(2, 1, 3, 0, 4)]
    transpose x2 -> x12, local copies, waits for them, and re-layouts: 2.44 us -> 7.89 us  [the longest x2 1.91 us: shards(): totals[256:1280].T.reshape(8, 32, 1024).transpose(1, 0, 2)]
  transfers between devices with their start and end apart: 8 -> 0, of which waited for: 8 -> 0; matrix products, arithmetic and copies ran while one was open for 14% -> 0% of each run, Pallas kernels for 0% -> 0%
where the time goes in v2:
time: 206 us
  Pallas kernels  178 us (86%)
  local copies, waits for them, and re-layouts  26.7 us (13%)
    pallas_call x1, Pallas kernels, shards(): pl.pallas_call(layer, name='monarch_layer', out_shape=(jax.ShapeDtypeStru...  178 us
    reshape x4, local copies, waits for them, and re-layouts, token_order(): values.reshape(8, 32, CHUNKS, per, 256).transpose(2, 1, 3, 0, 4)  5.79 us
    unnamed x18, local copies, waits for them, and re-layouts  4.26 us

profile of v2, /device:TPU:1, one launch (start us, length us, event | category | flops | bytes accessed | tf_op | source)
XLA Modules:
  0.0 205.6 jit_solution(3337241593087881502)
XLA Ops:
  0.7 0.9 copy.61
  1.5 0.7 copy.62
  2.2 1.7 copy.63
  3.9 1.6 copy.67
  5.4 1.0 copy.54
  6.6 0.7 reshape.81.mix_in
  7.2 0.9 reshape.82
  8.5 0.8 copy.59
  9.3 0.7 copy.60
  10.3 1.0 copy.65
  11.4 1.0 copy.66
  12.3 1.3 reshape.78
  13.7 2.1 %copy.53 = bf16[8,32,2,4,256]{4,0,3,1,2:T(8,128)(2,1)} copy(bf16[8,32,2,4,256]{4,3,2,1,0:T(4,128)(2,1)S(1)} %reshape.78) | data formatting | bytes 2097152 | tf_op jit(solution)/shard_map/reshape | solution.py:351
  16.1 2.1 %copy.52 = bf16[8,32,2,4,256]{4,0,3,1,2:T(8,128)(2,1)} copy(bf16[8,32,2,4,256]{4,3,2,1,0:T(4,128)(2,1)S(1)} %reshape.76) | data formatting | bytes 2097152 | tf_op jit(solution)/shard_map/reshape | solution.py:351
  18.2 177.9 %monarch_layer.1 = (bf16[2,1024,256]{2,1,0:T(8,128)(2,1)}, bf16[8,256,256]{2,1,0:T(8,128)(2,1)}, bf16[2560,256]{1,0:T(8,128)(2,1)}) custom-call(bf16[8,256,256]{2,1,0:T(8,128)(2,1)} %bitcast.65, bf16[2,1024,256]{2,1,0:T(8,128)(2,1)} %bitcast.67, bf16[2,1024,256]{2,1,0:T(8,128)(2,1)} %bitcast.66, bf16[256,256]{1,0:T(8,128)(2,1)} %reshape.81.mix_in, ...), custom_call_target="tpu_custom_call" | custom-call | tf_op jit(solution)/shard_map/monarch_layer/pallas_call | solution.py:363
  196.1 1.7 copy.69
  197.8 1.1 reshape.91
  199.2 0.4 copy.70
  199.6 1.1 reshape.93
  200.9 1.1 slice_bitcast_fusion
  202.0 0.9 copy.80
  202.9 0.8 copy.74
  203.7 0.3 copy.71
  204.0 1.6 copy.79
  (27 shorter events, 1.5 us)
Async XLA Ops:
  0.6 8.7 %copy-start.5 = (bf16[256,256]{1,0:T(8,128)(2,1)S(1)}, bf16[256,256]{1,0:T(8,128)(2,1)}, u32[]{:S(2)}) copy-start(bf16[256,256]{1,0:T(8,128)(2,1)} %mix_bwd.1) | copy-start | bytes 393220
  0.6 9.4 %copy-start.6 = (bf16[1,256,1024]{2,1,0:T(8,128)(2,1)S(1)}, bf16[1,256,1024]{2,1,0:T(8,128)(2,1)}, u32[]{:S(2)}) copy-start(bf16[1,256,1024]{2,1,0:T(8,128)(2,1)} %param.14) | copy-start | bytes 1572868
  6.4 4.9 %copy-start.2 = (bf16[1,1024,256]{2,1,0:T(8,128)(2,1)S(1)}, bf16[1,1024,256]{2,1,0:T(8,128)(2,1)}, u32[]{:S(2)}) copy-start(bf16[1,1024,256]{2,1,0:T(8,128)(2,1)} %param.15) | copy-start | bytes 1572868
  10.3 5.5 %copy-start = (bf16[8,32,1024]{2,1,0:T(8,128)(2,1)}, bf16[8,32,1024]{2,1,0:T(8,128)(2,1)S(1)}, u32[]{:S(2)}) copy-start(bf16[8,32,1024]{2,1,0:T(8,128)(2,1)S(1)} %copy.64) | copy-start | bytes 1572868
  11.3 4.4 %copy-start.1 = (bf16[2048,256]{1,0:T(8,128)(2,1)S(1)}, bf16[2048,256]{1,0:T(8,128)(2,1)}, u32[]{:S(2)}) copy-start(bf16[2048,256]{1,0:T(8,128)(2,1)} %param.9) | copy-start | bytes 3145732
  196.1 2.8 %copy-start.4 = (bf16[8,256,256]{2,1,0:T(8,128)(2,1)S(1)}, bf16[8,256,256]{2,1,0:T(8,128)(2,1)}, u32[]{:S(2)}) copy-start(bf16[8,256,256]{2,1,0:T(8,128)(2,1)} %get-tuple-element.10) | copy-start | bytes 3145732
  199.2 1.5 copy-start.3

commit v3 on v2

--- a/solution.py
+++ b/solution.py
@@ -11,7 +11,7 @@
 bf16, f32 = jnp.bfloat16, jnp.float32
 root_two_pi = 0.7978845608028654
 cubic_term = 0.044715
-CHUNKS = 2
+CHUNKS = 4
 A1, A2, A3, A4 = range(4)
 BACK, UP, GRAD, DOWN = range(4)
 
@@ -37,12 +37,13 @@
 
 
 def layer(
-    act_rows, act, gout, mix_in, mix_out, mix_fwd, mix_bwd, tw,
-    first_t, second, second_t, third, third_t, fourth,
-    out, grad_in, total,
+    act_rows, mix_first, twiddle, gout_any, mix_second_any, first_any, second_any, third_any, fourth_any,
+    out, tall_out, broad_out, grad_in,
+    gout_rows, mix_bwd, first, second_raw, third, fourth_raw,
+    act, gout, mix_fwd, first_t, second, second_t, third_t, fourth, total, out_v, tall_v, broad_v,
     wide, extra, field_s, field_r, swap_s, swap_r, hidden, active, gpre, acc, send_terms, half_in, half_sum,
     quarter_in, quarter_sum, last_in,
-    seq_send, seq_recv, swap_send, swap_recv, red_send, red_recv,
+    seq_send, seq_recv, swap_send, swap_recv, red_send, red_recv, load_sem, store_sem,
 ):
     s = lax.axis_index("seq")
     f = lax.axis_index("fsdp")
@@ -70,9 +71,10 @@
     def _(n):
         greet(s, (f + n) % 8)
 
-    def seq_start(phase, q):
-        pltpu.make_async_copy(field_s.at[phase, q, s], field_r.at[phase, q, s], seq_recv.at[phase, q]).start()
-        for dz in (2, 1, 3, 0):
+    def seq_start(phase, q, planes=(2, 1, 3, 0)):
+        if 0 in planes:
+            pltpu.make_async_copy(field_s.at[phase, q, s], field_r.at[phase, q, s], seq_recv.at[phase, q]).start()
+        for dz in planes:
             @pl.loop(1 if dz == 0 else 0, 8)
             def _(n):
                 peer = seq_peer(dz, n)
@@ -103,16 +105,45 @@
         whole = swap_r.at[phase, q]
         pltpu.make_async_copy(whole, whole, swap_recv.at[phase, q]).wait()
 
+    loads = [
+        pltpu.make_async_copy(source, target, load_sem.at[index])
+        for index, (source, target) in enumerate((
+            (gout_any, gout_rows), (fourth_any, fourth_raw), (mix_second_any, mix_bwd),
+            (first_any, first), (second_any, second_raw), (third_any, third),
+        ))
+    ]
+    for load in loads:
+        load.start()
+
+    row = lax.broadcasted_iota(jnp.int32, (256, 256), 0)
+    column = lax.broadcasted_iota(jnp.int32, (256, 256), 1)
+    one, zero = jnp.ones((256, 256), f32), jnp.zeros((256, 256), f32)
+    eye = jnp.where(row == column, one, zero).astype(bf16)
+    sort = jnp.where(column == (row % 32) * 8 + row // 32, one, zero).astype(bf16)
+    unsort = jnp.where(row == (column % 32) * 8 + column // 32, one, zero).astype(bf16)
+
+    def flip(values):
+        return nt(eye, values).astype(bf16)
+
+    def halves(values):
+        return [(half, values[:, half * 128 : half * 128 + 128]) for half in range(2)]
+
+    def interleave(index, values):
+        for half, part in halves(values):
+            wide[half, pl.ds(index, 256, stride=8), :] = part
+
+    def block_place(d, q):
+        return pl.ds(pl.multiple_of(d * 64 + q * rows, 8), rows)
+
+    tw = twiddle[...].T
+    mix_in = flip(mix_first[...])
     for a in range(8):
-        lines = nn(mix_in[...], act_rows[a]) * tw[:, a : a + 1]
-        for half in range(2):
-            wide[half, pl.ds(a, 256, stride=8), :] = lines[:, half * 128 : half * 128 + 128]
+        interleave(a, nn(mix_in, act_rows[a]) * tw[:, a : a + 1])
     for q in range(CHUNKS):
         @pl.loop(0, 32)
         def _(d):
             for half in range(2):
-                place = pl.ds(pl.multiple_of(q * 32 * rows + d * rows, 8), rows)
-                field_s[A1, q, d, :, half * 128 : half * 128 + 128] = wide[half, place, :].astype(bf16)
+                field_s[A1, q, d, :, half * 128 : half * 128 + 128] = wide[half, block_place(d, q), :].astype(bf16)
 
     pl.semaphore_wait(barrier, 38)
     for q in range(CHUNKS):
@@ -120,19 +151,49 @@
 
     tile = 256
     tiles = span // tile
+    per = tile // rows
 
     def token_tile(t):
         return pl.ds(pl.multiple_of(t * tile, tile), tile)
 
     def field_tile(ref, phase, q, t):
-        per = tile // rows
         return ref.at[phase, q, pl.ds(t * per, per)]
 
+    def token_order(source, target):
+        for a in range(8):
+            interleave(a, source[a].astype(f32))
+        for q in range(CHUNKS):
+            @pl.loop(0, 32)
+            def _(d):
+                place = pl.ds(pl.multiple_of(d * rows, rows), rows)
+                for half in range(2):
+                    target[q, place, half * 128 : half * 128 + 128] = wide[half, block_place(d, q), :].astype(bf16)
+
+    def scatter(target, q, t, values):
+        for half, part in halves(values):
+            for n in range(per):
+                target[half, block_place(t * per + n, q), :] = part[n * rows : (n + 1) * rows]
+
+    loads[0].wait()
+    token_order(gout_rows, gout)
+    loads[1].wait()
+    fourth[...] = nn(sort, fourth_raw[...]).astype(bf16)
     for q in range(CHUNKS):
         @pl.loop(0, tiles)
         def _(t):
             swap_s[BACK, q, :, token_tile(t)] = nt(fourth[...], gout[q, token_tile(t), :]).astype(bf16)
         swap_start(BACK, q)
+    token_order(act_rows, act)
+    for load in loads[2:]:
+        load.wait()
+    mix_fwd[...] = flip(mix_bwd[...])
+    first_t[...] = flip(first[...])
+    for o in range(4):
+        units = pl.ds(o * 256, 256)
+        sorted_units = nn(sort, second_raw[:, units]).astype(bf16)
+        second[:, units] = sorted_units
+        second_t[units, :] = flip(sorted_units)
+        third_t[:, units] = flip(third[units, :])
 
     def mix_columns(source, target, factor, q):
         for pair in range(rows // 16):
@@ -160,6 +221,12 @@
             hidden[q, token_tile(t), :] = rows_hidden
             swap_s[UP, q, :, token_tile(t)] = nt(first_t[...], rows_hidden).astype(bf16)
         swap_start(UP, q)
+
+    def add(place, values, q):
+        if q == 0:
+            acc[place, :] = values
+        else:
+            acc[place, :] += values
 
     for q in range(CHUNKS):
         if q == 0:
@@ -180,11 +247,21 @@
                 active[q, units, columns] = value.astype(bf16)
                 gpre[q, units, columns] = (nn(third[units, :], back) * slope).astype(bf16)
             swap_s[GRAD, q, :, columns] = nn(second[...], gpre[q, :, columns]).astype(bf16)
+        swap_start(GRAD, q)
+
+        @pl.loop(0, tiles)
+        def _(t):
+            columns = token_tile(t)
             swap_s[DOWN, q, :, columns] = nn(third_t[...], active[q, :, columns]).astype(bf16)
-        swap_start(GRAD, q)
         swap_start(DOWN, q)
 
-    for q in range(CHUNKS):
+        @pl.loop(0, 4)
+        def _(o):
+            units = pl.ds(pl.multiple_of(o * 256, 256), 256)
+            add(pl.ds(pl.multiple_of(256 + o * 256, 256), 256), nt(gpre[q, units, :], swap_r[UP, q]), q)
+            add(pl.ds(pl.multiple_of(1280 + o * 256, 256), 256), nt(active[q, units, :], swap_r[BACK, q]), q)
+
+    def back_rows(q):
         swap_wait(GRAD, q)
 
         @pl.loop(0, tiles)
@@ -194,34 +271,19 @@
             back = (gout[q, columns, :].astype(f32) + inner).astype(bf16).astype(f32)
             gating = jax.nn.sigmoid(gate(q, t))
             mixed = field_tile(field_r, A2, q, t)[...].reshape(tile, 256).astype(f32)
-            field_tile(field_s, A3, q, t)[...] = (back * gating).astype(bf16).reshape(tile // rows, rows, 256)
+            field_tile(field_s, A3, q, t)[...] = (back * gating).astype(bf16).reshape(per, rows, 256)
             rest = back * (1.0 + gating * (1.0 - gating) * mixed)
-            for half in range(2):
-                place = pl.ds(pl.multiple_of(q * span + t * tile, tile), tile)
-                extra[half, place, :] = rest[:, half * 128 : half * 128 + 128]
-        seq_start(A3, q)
-
-    def add(place, values, q):
-        if q == 0:
-            acc[place, :] = values
-        else:
-            acc[place, :] += values
-
-    for q in range(CHUNKS):
-        @pl.loop(0, 4)
-        def _(o):
-            units = pl.ds(pl.multiple_of(o * 256, 256), 256)
-            add(pl.ds(pl.multiple_of(256 + o * 256, 256), 256), nt(gpre[q, units, :], swap_r[UP, q]), q)
-            add(pl.ds(pl.multiple_of(1280 + o * 256, 256), 256), nt(active[q, units, :], swap_r[BACK, q]), q)
+            scatter(extra, q, t, rest)
+
+    def out_rows(q):
+        @pl.loop(0, tiles)
+        def _(t):
+            columns = token_tile(t)
+            scatter(wide, q, t, hidden[q, columns, :].astype(f32) + tn(swap_r[DOWN, q, :, columns], fourth[...]))
+
+    def last_terms(q):
         add(pl.ds(0, 256), nn(swap_r[GRAD, q], hidden[q]), q)
-
-    for q in range(CHUNKS):
         swap_wait(DOWN, q)
-
-        @pl.loop(0, tiles)
-        def _(t):
-            columns = token_tile(t)
-            out[q, columns, :] = (hidden[q, columns, :].astype(f32) + tn(swap_r[DOWN, q, :, columns], fourth[...])).astype(bf16)
         add(pl.ds(2304, 256), nn(swap_r[DOWN, q], gout[q]), q)
 
     def core_peer():
@@ -300,19 +362,46 @@
         for copy in copies:
             copy.wait()
 
+    final = CHUNKS - 1
+    for q in range(final):
+        back_rows(q)
+        seq_start(A3, q)
+        last_terms(q)
+    back_rows(final)
+    last_terms(final)
     copies = reduce_core()
+    seq_start(A3, final, (2,))
+    out_rows(0)
+    finish(copies)
+    copies = reduce_x()
+    seq_start(A3, final, (1, 3, 0))
+    for q in range(1, CHUNKS):
+        out_rows(q)
+    for a in range(8):
+        for half in range(2):
+            out_v[a, :, half * 128 : half * 128 + 128] = wide[half, pl.ds(a, 256, stride=8), :].astype(bf16)
+    stores = [pltpu.make_async_copy(out_v, out, store_sem.at[0])]
+    stores[0].start()
+
+    steps = [reduce_z, gather_z, gather_x, gather_core]
     for q in range(CHUNKS):
         seq_wait(A3, q)
         mix_columns(A3, A4, mix_bwd, q)
-        seq_start(A4, q)
-        if q == 0:
-            finish(copies)
-            copies = reduce_x()
+        parts = ((2, 1, 3, 0),) if q < final else ((2,), (1,), (3, 0))
+        for part in parts:
+            if steps:
+                finish(copies)
+                copies = steps.pop(0)()
+            seq_start(A4, q, part)
     finish(copies)
-    finish(reduce_z())
-    finish(gather_z())
-    finish(gather_x())
-    copies = gather_core()
+    tall_v[0:256, :] = flip(total[0:256, :])
+    tall_v[256:1280, :] = total[1280:2304, :]
+    tall_v[1280:1536, :] = nn(unsort, total[2304:2560, :]).astype(bf16)
+    for o in range(4):
+        broad_v[:, o * 256 : o * 256 + 256] = nt(unsort, total[256 + o * 256 : 512 + o * 256, :]).astype(bf16)
+    for n, (source, target) in enumerate(((tall_v, tall_out), (broad_v, broad_out))):
+        stores.append(pltpu.make_async_copy(source, target, store_sem.at[n + 1]))
+        stores[-1].start()
 
     for q in range(CHUNKS):
         seq_wait(A4, q)
@@ -320,15 +409,15 @@
         @pl.loop(0, 32)
         def _(d):
             for half in range(2):
-                place = pl.ds(pl.multiple_of(q * 32 * rows + d * rows, 8), rows)
-                wide[half, place, :] = field_r[A4, q, d, :, half * 128 : half * 128 + 128].astype(f32)
+                wide[half, block_place(d, q), :] = field_r[A4, q, d, :, half * 128 : half * 128 + 128].astype(f32)
     for a in range(8):
         lines = pl.ds(a, 256, stride=8)
         for half in range(2):
             twisted = (wide[half, lines, :] * tw[:, a : a + 1]).astype(bf16)
-            grad_in[a, :, half * 128 : half * 128 + 128] = (extra[half, lines, :] + nn(mix_out[...], twisted)).astype(bf16)
-    finish(copies)
-
+            grad_in[a, :, half * 128 : half * 128 + 128] = (extra[half, lines, :] + nn(mix_first[...], twisted)).astype(bf16)
+
+    for store in stores:
+        store.wait()
     for q in range(CHUNKS):
         for phase in range(4):
             sent = field_s.at[phase, q, pl.ds(0, 31)]
@@ -338,39 +427,36 @@
 
 
 def shards(activations, mix_first, twiddle, mix_second, up_first, up_second, down_first, down_second, grad_out):
-    per = 8 // CHUNKS
     span = 2048 // CHUNKS
-    first, second, third, fourth = up_first[0], up_second[0], down_first[0], down_second[0]
-    second = second.reshape(32, 8, 1024).transpose(1, 0, 2).reshape(256, 1024)
-    fourth = fourth.reshape(32, 8, 256).transpose(1, 0, 2).reshape(256, 256)
-
-    def reorder(values):
-        return values.reshape(32, CHUNKS, per, -1).transpose(1, 0, 2, 3).reshape(256, -1)
-
-    def token_order(values):
-        return values.reshape(8, 32, CHUNKS, per, 256).transpose(2, 1, 3, 0, 4).reshape(CHUNKS, span, 256)
-
-    mix_in = reorder(mix_first.T)
-    mix_out = reorder(reorder(mix_first).T).T
-    tw = reorder(twiddle.T)
-    act_rows = activations.reshape(8, 256, 256)
     args = (
-        act_rows, token_order(activations), token_order(grad_out), mix_in, mix_out, mix_second.T, mix_second, tw,
-        first.T, second, second.T, third, third.T, fourth,
+        activations.reshape(8, 256, 256), mix_first, twiddle, grad_out.reshape(8, 256, 256), mix_second,
+        up_first[0], up_second[0], down_first[0], down_second[0],
     )
     vmem = pl.BlockSpec(memory_space=pltpu.VMEM)
     rows = 64 // CHUNKS
-    output, grad_in, total = pl.pallas_call(
+    square = pltpu.VMEM((256, 256), bf16)
+    broad, tall = pltpu.VMEM((256, 1024), bf16), pltpu.VMEM((1024, 256), bf16)
+    output, tall_sums, broad_sums, grad_in = pl.pallas_call(
         layer,
         name="monarch_layer",
         out_shape=(
-            jax.ShapeDtypeStruct((CHUNKS, span, 256), bf16),
             jax.ShapeDtypeStruct((8, 256, 256), bf16),
-            jax.ShapeDtypeStruct((2560, 256), bf16),
+            jax.ShapeDtypeStruct((1536, 256), bf16),
+            jax.ShapeDtypeStruct((256, 1024), bf16),
+            jax.ShapeDtypeStruct((8, 256, 256), bf16),
         ),
-        in_specs=[vmem] * len(args),
-        out_specs=(vmem,) * 3,
+        in_specs=[vmem] * 3 + [pl.BlockSpec(memory_space=pl.ANY)] * 6,
+        out_specs=(pl.BlockSpec(memory_space=pl.ANY),) * 3 + (vmem,),
         scratch_shapes=[
+            pltpu.VMEM((8, 256, 256), bf16),
+            square, square, broad, tall, square,
+            pltpu.VMEM((CHUNKS, span, 256), bf16),
+            pltpu.VMEM((CHUNKS, span, 256), bf16),
+            square, square, broad, tall, broad, square,
+            pltpu.VMEM((2560, 256), bf16),
+            pltpu.VMEM((8, 256, 256), bf16),
+            pltpu.VMEM((1536, 256), bf16),
+            broad,
             pltpu.VMEM((2, 2048, 128), f32),
             pltpu.VMEM((2, 2048, 128), f32),
             pltpu.VMEM((4, CHUNKS, 32, rows, 256), bf16),
@@ -393,18 +479,18 @@
             pltpu.SemaphoreType.DMA((4, CHUNKS)),
             pltpu.SemaphoreType.DMA((6, 3)),
             pltpu.SemaphoreType.DMA((6, 3)),
+            pltpu.SemaphoreType.DMA((6,)),
+            pltpu.SemaphoreType.DMA((3,)),
         ],
         compiler_params=pltpu.CompilerParams(collective_id=0, has_side_effects=True, vmem_limit_bytes=60 << 20),
     )(*args)
 
-    output = output.reshape(CHUNKS, 32, per, 8, 256).transpose(3, 1, 0, 2, 4).reshape(2048, 256)
-    grad_in = grad_in.reshape(8, CHUNKS, 32, per, 256).transpose(0, 2, 1, 3, 4).reshape(2048, 256)
-    totals = total.astype(f32) * (1.0 / 256)
-    sum_first = totals[:256].T
-    sum_second = totals[256:1280].T.reshape(8, 32, 1024).transpose(1, 0, 2).reshape(256, 1024)
-    sum_third = totals[1280:2304]
-    sum_fourth = totals[2304:].reshape(8, 32, 256).transpose(1, 0, 2).reshape(256, 256)
-    return (output, grad_in, sum_first[None], sum_second[None], sum_third[None], sum_fourth[None])
+    tall_sums = tall_sums.astype(f32) * (1.0 / 256)
+    broad_sums = broad_sums.astype(f32) * (1.0 / 256)
+    return (
+        output.reshape(2048, 256), grad_in.reshape(2048, 256),
+        tall_sums[None, :256], broad_sums[None], tall_sums[None, 256:1280], tall_sums[None, 1280:],
+    )
 
 
 def solution(mesh):

time: 206 us -> 177 us (0.86)
  local copies, waits for them, and re-layouts: 26.7 us -> 3.81 us
  Pallas kernels: 178 us -> 170 us
  other arithmetic: 0.17 us -> 2.33 us
    reshape x16 -> x0, local copies, waits for them, and re-layouts: 11.9 us -> none  [the longest x4 5.79 us: token_order(): values.reshape(8, 32, CHUNKS, per, 256).transpose(2, 1, 3, 0, 4)]
    pallas_call x1, Pallas kernels: 178 us -> 170 us  [shards(): pl.pallas_call(layer, name='monarch_layer', out_shape=(jax.ShapeDtypeStru...]
    transpose x12 -> x0, local copies, waits for them, and re-layouts: 7.89 us -> none  [the longest x2 1.91 us: shards(): totals[256:1280].T.reshape(8, 32, 1024).transpose(1, 0, 2)]
    unnamed x18 -> x8, local copies, waits for them, and re-layouts: 4.26 us -> 1.95 us
where the time goes in v3:
time: 177 us
  Pallas kernels  170 us (96%)
  local copies, waits for them, and re-layouts  3.81 us (2%)
  other arithmetic  2.33 us (1%)
    pallas_call x1, Pallas kernels, shards(): pl.pallas_call(layer, name='monarch_layer', out_shape=(jax.ShapeDtypeStru...  170 us

profile of v3, /device:TPU:1, one launch (start us, length us, event | category | flops | bytes accessed | tf_op | source)
XLA Modules:
  0.0 176.6 jit_solution(886611010225684121)
XLA Ops:
  0.6 169.8 %monarch_layer.1 = (bf16[8,256,256]{2,1,0:T(8,128)(2,1)}, bf16[1536,256]{1,0:T(8,128)(2,1)}, bf16[256,1024]{1,0:T(8,128)(2,1)}, bf16[8,256,256]{2,1,0:T(8,128)(2,1)}) custom-call(bf16[8,256,256]{2,1,0:T(8,128)(2,1)} %bitcast.16, bf16[256,256]{1,0:T(8,128)(2,1)} %mix_first.1, f32[8,256]{1,0:T(8,128)} %twiddle.1, bf16[8,256,256]{2,1,0:T(8,128)(2,1)} %bitcast.17, ...), custom_call_target="tpu_custom_call" | custom-call | tf_op jit(solution)/shard_map/monarch_layer/pallas_call | solution.py:439
  170.4 1.2 convert_multiply_fusion
  171.7 0.0 copy-start.2
  171.7 0.8 slice_bitcast_fusion.1
  172.5 0.0 copy-start.1
  172.5 1.0 slice_bitcast_fusion
  173.5 0.0 copy-done.2
  173.5 0.0 copy-start
  173.5 1.1 multiply_bitcast_fusion
  174.6 0.0 copy-done.1
  174.6 1.0 copy.17
  175.6 0.0 copy-done
  175.6 1.0 copy.18
Async XLA Ops:
  171.7 1.9 %copy-start.2 = (bf16[256,1024]{1,0:T(8,128)(2,1)S(1)}, bf16[256,1024]{1,0:T(8,128)(2,1)}, u32[]{:S(2)}) copy-start(bf16[256,1024]{1,0:T(8,128)(2,1)} %get-tuple-element.13) | copy-start | bytes 1572868
  172.5 2.1 %copy-start.1 = (bf16[8,256,256]{2,1,0:T(8,128)(2,1)S(1)}, bf16[8,256,256]{2,1,0:T(8,128)(2,1)}, u32[]{:S(2)}) copy-start(bf16[8,256,256]{2,1,0:T(8,128)(2,1)} %get-tuple-element.10) | copy-start | bytes 3145732
  173.5 2.1 %copy-start = (bf16[8,256,256]{2,1,0:T(8,128)(2,1)S(1)}, bf16[8,256,256]{2,1,0:T(8,128)(2,1)}, u32[]{:S(2)}) copy-start(bf16[8,256,256]{2,1,0:T(8,128)(2,1)} %get-tuple-element.11) | copy-start | bytes 3145732

commit v4 on v3

--- a/solution.py
+++ b/solution.py
@@ -75,7 +75,7 @@
         if 0 in planes:
             pltpu.make_async_copy(field_s.at[phase, q, s], field_r.at[phase, q, s], seq_recv.at[phase, q]).start()
         for dz in planes:
-            @pl.loop(1 if dz == 0 else 0, 8)
+            @pl.loop(1 if dz == 0 else 0, 8, unroll=True)
             def _(n):
                 peer = seq_peer(dz, n)
                 pltpu.make_async_remote_copy(
@@ -92,7 +92,7 @@
         own = pl.ds(pl.multiple_of(f * 32, 32), 32)
         pltpu.make_async_copy(swap_s.at[phase, q, own], swap_r.at[phase, q, own], swap_recv.at[phase, q]).start()
 
-        @pl.loop(1, 8)
+        @pl.loop(1, 8, unroll=True)
         def _(n):
             peer = swap_peer(8 - n)
             pltpu.make_async_remote_copy(
@@ -240,7 +240,7 @@
             up = swap_r[UP, q, :, columns]
             back = swap_r[BACK, q, :, columns]
 
-            @pl.loop(0, 4)
+            @pl.loop(0, 4, unroll=True)
             def _(o):
                 units = pl.ds(pl.multiple_of(o * 256, 256), 256)
                 value, slope = gelu_both(nn(second_t[units, :], up))
@@ -249,13 +249,13 @@
             swap_s[GRAD, q, :, columns] = nn(second[...], gpre[q, :, columns]).astype(bf16)
         swap_start(GRAD, q)
 
-        @pl.loop(0, tiles)
+        @pl.loop(0, tiles, unroll=True)
         def _(t):
             columns = token_tile(t)
             swap_s[DOWN, q, :, columns] = nn(third_t[...], active[q, :, columns]).astype(bf16)
         swap_start(DOWN, q)
 
-        @pl.loop(0, 4)
+        @pl.loop(0, 4, unroll=True)
         def _(o):
             units = pl.ds(pl.multiple_of(o * 256, 256), 256)
             add(pl.ds(pl.multiple_of(256 + o * 256, 256), 256), nt(gpre[q, units, :], swap_r[UP, q]), q)
@@ -424,6 +424,39 @@
             pltpu.make_async_copy(sent, sent, seq_send.at[phase, q]).wait()
             sent = swap_s.at[phase, q, pl.ds(0, 224)]
             pltpu.make_async_copy(sent, sent, swap_send.at[phase, q]).wait()
+
+
+def hand_out(
+    rows_in, grad_in, tall_in, broad_in, rows_out, grad_out, first, second, third, fourth,
+    rows_v, grad_v, tall_v, broad_v, tall_f, broad_f, load_sem, store_sem,
+):
+    loads = [
+        pltpu.make_async_copy(source, target, load_sem.at[n])
+        for n, (source, target) in enumerate(((tall_in, tall_v), (broad_in, broad_v), (rows_in, rows_v), (grad_in, grad_v)))
+    ]
+    for load in loads:
+        load.start()
+    stores = []
+
+    def store(source, target):
+        stores.append(pltpu.make_async_copy(source, target, store_sem.at[len(stores)]))
+        stores[-1].start()
+
+    scale = 1.0 / 256
+    loads[0].wait()
+    tall_f[...] = tall_v[...].astype(f32) * scale
+    store(tall_f.at[pl.ds(0, 256)], first)
+    store(tall_f.at[pl.ds(256, 1024)], third)
+    store(tall_f.at[pl.ds(1280, 256)], fourth)
+    loads[1].wait()
+    broad_f[...] = broad_v[...].astype(f32) * scale
+    store(broad_f, second)
+    loads[2].wait()
+    store(rows_v, rows_out)
+    loads[3].wait()
+    store(grad_v, grad_out)
+    for copy in stores:
+        copy.wait()
 
 
 def shards(activations, mix_first, twiddle, mix_second, up_first, up_second, down_first, down_second, grad_out):
@@ -485,11 +518,35 @@
         compiler_params=pltpu.CompilerParams(collective_id=0, has_side_effects=True, vmem_limit_bytes=60 << 20),
     )(*args)
 
-    tall_sums = tall_sums.astype(f32) * (1.0 / 256)
-    broad_sums = broad_sums.astype(f32) * (1.0 / 256)
+    anywhere = pl.BlockSpec(memory_space=pl.ANY)
+    output, grad_in, sum_first, sum_second, sum_third, sum_fourth = pl.pallas_call(
+        hand_out,
+        name="hand_out",
+        out_shape=(
+            jax.ShapeDtypeStruct((8, 256, 256), bf16),
+            jax.ShapeDtypeStruct((8, 256, 256), bf16),
+            jax.ShapeDtypeStruct((256, 256), f32),
+            jax.ShapeDtypeStruct((256, 1024), f32),
+            jax.ShapeDtypeStruct((1024, 256), f32),
+            jax.ShapeDtypeStruct((256, 256), f32),
+        ),
+        in_specs=[anywhere] * 4,
+        out_specs=(anywhere,) * 6,
+        scratch_shapes=[
+            pltpu.VMEM((8, 256, 256), bf16),
+            pltpu.VMEM((8, 256, 256), bf16),
+            pltpu.VMEM((1536, 256), bf16),
+            broad,
+            pltpu.VMEM((1536, 256), f32),
+            pltpu.VMEM((256, 1024), f32),
+            pltpu.SemaphoreType.DMA((4,)),
+            pltpu.SemaphoreType.DMA((6,)),
+        ],
+        compiler_params=pltpu.CompilerParams(vmem_limit_bytes=60 << 20),
+    )(output, grad_in, tall_sums, broad_sums)
     return (
         output.reshape(2048, 256), grad_in.reshape(2048, 256),
-        tall_sums[None, :256], broad_sums[None], tall_sums[None, 256:1280], tall_sums[None, 1280:],
+        sum_first[None], sum_second[None], sum_third[None], sum_fourth[None],
     )
 
 

time: 177 us -> 174 us (0.983)
  local copies, waits for them, and re-layouts: 3.81 us -> 0 us
  Pallas kernels: 170 us -> 173 us
  other arithmetic: 2.33 us -> 0 us
    pallas_call x0 -> x1, Pallas kernels: none -> 3.5 us  [shards(): pl.pallas_call(hand_out, name='hand_out', out_shape=(jax.ShapeDtypeStruct...]
    unnamed x8 -> x0, local copies, waits for them, and re-layouts: 1.95 us -> none
    broadcast_in_dim x2 -> x0, local copies, waits for them, and re-layouts: 1.86 us -> none  [the longest x1 1.04 us: shards(): tall_sums[None, 256:1280]]
where the time goes in v4:
time: 174 us
  Pallas kernels  173 us (99%)
    pallas_call x1, Pallas kernels, shards(): pl.pallas_call(layer, name='monarch_layer', out_shape=(jax.ShapeDtypeStru...  170 us
    pallas_call x1, Pallas kernels, shards(): pl.pallas_call(hand_out, name='hand_out', out_shape=(jax.ShapeDtypeStruct...  3.5 us

profile of v4, /device:TPU:1, one launch (start us, length us, event | category | flops | bytes accessed | tf_op | source)
XLA Modules:
  0.0 173.9 jit_solution(4167420118817839198)
XLA Ops:
  0.6 169.5 %monarch_layer.1 = (bf16[8,256,256]{2,1,0:T(8,128)(2,1)}, bf16[1536,256]{1,0:T(8,128)(2,1)}, bf16[256,1024]{1,0:T(8,128)(2,1)}, bf16[8,256,256]{2,1,0:T(8,128)(2,1)}) custom-call(bf16[8,256,256]{2,1,0:T(8,128)(2,1)} %bitcast.12, bf16[256,256]{1,0:T(8,128)(2,1)} %mix_first.1, f32[8,256]{1,0:T(8,128)} %twiddle.1, bf16[8,256,256]{2,1,0:T(8,128)(2,1)} %bitcast.13, ...), custom_call_target="tpu_custom_call" | custom-call | tf_op jit(solution)/shard_map/monarch_layer/pallas_call | solution.py:472
  170.2 3.5 %hand_out.1 = (bf16[8,256,256]{2,1,0:T(8,128)(2,1)}, bf16[8,256,256]{2,1,0:T(8,128)(2,1)}, f32[256,256]{1,0:T(8,128)}, f32[256,1024]{1,0:T(8,128)}, f32[1024,256]{1,0:T(8,128)}, /*index=5*/f32[256,256]{1,0:T(8,128)}) custom-call(bf16[8,256,256]{2,1,0:T(8,128)(2,1)} %get-tuple-element.16.rows_in, bf16[8,256,256]{2,1,0:T(8,128)(2,1)} %get-tuple-element.17.grad_in, ...), custom_call_target="tpu_custom_call" | custom-call | tf_op jit(solution)/shard_map/hand_out/pallas_call | solution.py:522

commit v5 on v4

--- a/solution.py
+++ b/solution.py
@@ -74,15 +74,22 @@
     def seq_start(phase, q, planes=(2, 1, 3, 0)):
         if 0 in planes:
             pltpu.make_async_copy(field_s.at[phase, q, s], field_r.at[phase, q, s], seq_recv.at[phase, q]).start()
+        def send(dz, n):
+            peer = seq_peer(dz, n)
+            pltpu.make_async_remote_copy(
+                src_ref=field_s.at[phase, q, peer], dst_ref=field_r.at[phase, q, s],
+                send_sem=seq_send.at[phase, q], recv_sem=seq_recv.at[phase, q],
+                device_id={"seq": peer, "fsdp": f}, device_id_type=MESH,
+            ).start()
+
         for dz in planes:
-            @pl.loop(1 if dz == 0 else 0, 8, unroll=True)
-            def _(n):
-                peer = seq_peer(dz, n)
-                pltpu.make_async_remote_copy(
-                    src_ref=field_s.at[phase, q, peer], dst_ref=field_r.at[phase, q, s],
-                    send_sem=seq_send.at[phase, q], recv_sem=seq_recv.at[phase, q],
-                    device_id={"seq": peer, "fsdp": f}, device_id_type=MESH,
-                ).start()
+            if dz:
+                send(dz, 0)
+
+        @pl.loop(1, 8, unroll=True)
+        def _(n):
+            for dz in planes:
+                send(dz, n)
 
     def seq_wait(phase, q):
         whole = field_r.at[phase, q]

time: 174 us -> 174 us (level)
  no operation moved by 1% of the time
where the time goes in v5:
time: 174 us
  Pallas kernels  173 us (99%)
    pallas_call x1, Pallas kernels, shards(): pl.pallas_call(layer, name='monarch_layer', out_shape=(jax.ShapeDtypeStru...  169 us
    pallas_call x1, Pallas kernels, shards(): pl.pallas_call(hand_out, name='hand_out', out_shape=(jax.ShapeDtypeStruct...  3.5 us

profile of v5, /device:TPU:1, one launch (start us, length us, event | category | flops | bytes accessed | tf_op | source)
XLA Modules:
  0.0 173.7 jit_solution(5498183689250754139)
XLA Ops:
  0.6 169.4 %monarch_layer.1 = (bf16[8,256,256]{2,1,0:T(8,128)(2,1)}, bf16[1536,256]{1,0:T(8,128)(2,1)}, bf16[256,1024]{1,0:T(8,128)(2,1)}, bf16[8,256,256]{2,1,0:T(8,128)(2,1)}) custom-call(bf16[8,256,256]{2,1,0:T(8,128)(2,1)} %bitcast.12, bf16[256,256]{1,0:T(8,128)(2,1)} %mix_first.1, f32[8,256]{1,0:T(8,128)} %twiddle.1, bf16[8,256,256]{2,1,0:T(8,128)(2,1)} %bitcast.13, ...), custom_call_target="tpu_custom_call" | custom-call | tf_op jit(solution)/shard_map/monarch_layer/pallas_call | solution.py:479
  170.0 3.5 %hand_out.1 = (bf16[8,256,256]{2,1,0:T(8,128)(2,1)}, bf16[8,256,256]{2,1,0:T(8,128)(2,1)}, f32[256,256]{1,0:T(8,128)}, f32[256,1024]{1,0:T(8,128)}, f32[1024,256]{1,0:T(8,128)}, /*index=5*/f32[256,256]{1,0:T(8,128)}) custom-call(bf16[8,256,256]{2,1,0:T(8,128)(2,1)} %get-tuple-element.16.rows_in, bf16[8,256,256]{2,1,0:T(8,128)(2,1)} %get-tuple-element.17.grad_in, ...), custom_call_target="tpu_custom_call" | custom-call | tf_op jit(solution)/shard_map/hand_out/pallas_call | solution.py:529
